TPU v7x, 256 devices: a whole 4x4x8 slice. The times are simulated.
256 devices in a mesh: group: 4 (over y), dom: 64 (over z, x, core).
Axes of the slice: x: 4, y: 4, z: 8, core: 2. Of those that a mesh axis runs over, the one named last changes fastest.
Arguments:
- feats: bfloat16 [65536, 512], P(('group', 'dom')), may hold values from -6 to 6
- neigh: bfloat16 [65536, 512], P(('group', 'dom')), may hold values from -6 to 6
- pre_act: bfloat16 [65536, 512], P(('group', 'dom')), may hold values from -6 to 6
- cotan: bfloat16 [65536, 512], P(('group', 'dom')), may hold values from -6 to 6
- w_self: bfloat16 [512, 512], replicated, may hold values from -0.25 to 0.25
- w_neigh: bfloat16 [512, 512], replicated, may hold values from -0.25 to 0.25
- send_list: int32 [4, 64, 64], P('group', 'dom'), may hold values from 0 to 1
- send_live: int32 [4, 64, 64], P('group', 'dom'), may hold values 0 or 1
- cross_list: int32 [4, 64, 4, 2], P('group', 'dom'), may hold values from 0 to 1
- cross_live: int32 [4, 64, 4, 2], P('group', 'dom'), may hold values 0 or 1
- home_tiles: bfloat16 [4, 64, 16, 128, 128], P('group', 'dom'), may hold values from 0 to 0.039794922
- home_target: int32 [4, 64, 16], P('group', 'dom'), may hold values from 0 to 1
- home_source: int32 [4, 64, 16], P('group', 'dom'), may hold values from 0 to 73
- far_tiles: bfloat16 [4, 64, 16, 128, 128], P('group', 'dom'), may hold values from 0 to 0.039794922
- far_target: int32 [4, 64, 16], P('group', 'dom'), may hold values from 2 to 73
- far_source: int32 [4, 64, 16], P('group', 'dom'), may hold values from 0 to 73
- far_count: int32 [4, 64], P('group', 'dom'), may hold values from 1 to 16, as said below
Outputs:
- grad_input: bfloat16 [65536, 512], P(('group', 'dom'))
- grad_wself: float32 [512, 512], replicated
- grad_wneigh: float32 [512, 512], replicated
- grad_bias: float32 [512], replicated
Inputs may be any that keep to these rules, and one draw needn't show every extreme that they name: `far_count`: some partition uses all 16 far tiles.
All inputs are finite; a program needn't handle non-finite values. No bound on the sum of `send_live` or of `cross_live` on one device may be relied on, other than what follows from the above.
Results may differ from a plain program's by a relative error of at most 0.0045.
Values may be sent and summed in bfloat16 or wider, within the bound.
No kernel may reach another device: no remote copies, remote signals or barrier semaphores. Data moves between devices by JAX's collectives and lax.ppermute only.
A program may use at most 128 MiB of HBM per device.

v0:
```python
import jax
import jax.numpy as jnp
from jax import lax
from jax.experimental import pallas as pl
from jax.experimental.pallas import tpu as pltpu
from jax.sharding import Mesh
from jax.sharding import PartitionSpec as P

AXES = ("group", "z", "x", "core")
DOM = ("z", "x", "core")
NY, NZ, NX = 4, 8, 4
BLK, HALF = 128, 256
NT = 16
SLOTS = 32
bf16, f32, i32 = jnp.bfloat16, jnp.float32, jnp.int32

SEND, CROSS, HT, HS, FT, FS, FC, INTS = 0, 64, 72, 88, 104, 120, 136, 256
HEAD = 16
FIELDS, ENTRIES = 5, 160
LIST = 1 + FIELDS * ENTRIES
PICKED = 1 + 128

GROUPS = (
    ((0, 8), (8, 8), (16, 4), (20, 4), (24, 8), (32, 8)),
    ((0, 16), (16, 16), (32, 8), (40, 8), (48, 16), (64, 16)),
    ((0, 16), (16, 8), (24, 8), (32, 8), (40, 8), (48, 8)),
)
STARTS, SIZES = (0, 40, 120), (40, 80, 56)
MIB = 2**20

VMEM = pl.BlockSpec(memory_space=pltpu.VMEM)
SMEM = pl.BlockSpec(memory_space=pltpu.SMEM)
ANY = pl.BlockSpec(memory_space=pl.ANY)
HBM = pl.BlockSpec(memory_space=pltpu.HBM)


def shift(value, axis, k):
    n = {"group": NY, "z": NZ, "x": NX, "core": 2}[axis]
    return lax.ppermute(value, axis, [(i, (i + k) % n) for i in range(n)])


def pick_kernel(meta, row, out):
    x = meta[2]
    out[0] = 0
    for dx in range(NX):
        for r in range(2):
            base = (dx * 2 + r) * INTS

            @pl.loop(0, jnp.minimum(row[base + FC], NT))
            def _(t, dx=dx, r=r, base=base):
                slot = row[base + FT + t]
                column = ((slot - 2) >> 1) & 3
                here = jnp.where(slot < 66, column == x, dx == 0)

                @pl.when(here)
                def _():
                    n = out[0]
                    out[0] = n + 1
                    out[1 + n] = (dx * 2 + r) * NT + t


def list_kernel(meta, row, picked, *refs):
    heads, lists, (low, wide, words, sems) = refs[:11], refs[11:14], refs[14:]
    core, z, x, y = (meta[j] for j in range(4))
    copies = [pltpu.make_async_copy(v.at[pl.ds(0, HEAD)], low.at[j], sems.at[j]) for j, v in enumerate(heads)]
    for copy in copies:
        copy.start()
    for copy in copies:
        copy.wait()
    wide[...] = low[...].astype(f32).astype(i32)
    copy = pltpu.make_async_copy(wide.at[:, pl.ds(0, 8)], words, sems.at[0])
    copy.start()
    copy.wait()
    for out in lists:
        out[0] = 0

    def master(slot, dx, r):
        in_dom = slot < 66
        q = jnp.clip(slot - 2, 0, 63)
        dz = ((q >> 3) - z) & 7
        to_x = (((q >> 1) & 3) - x) & 3
        same = ((q & 1) ^ core)
        me = z * 8 + ((x + dx) & 3) * 2 + (core ^ r)
        v = jnp.clip(slot - 66, 0, 7)
        dy = ((v >> 1) - y) & 3
        word = jnp.where(
            in_dom,
            words[dz, to_x >> 1, ((to_x & 1) * 2 + same) * 64 + me],
            words[jnp.where(dy == 0, 0, 11 - dy), 2, (dx * 2 + r) * 8 + y * 2 + (v & 1)],
        )
        k = word & 1
        dz = jnp.where(in_dom, dz, 0)
        to_x = jnp.where(in_dom, to_x, dx)
        same = jnp.where(in_dom, same, r)
        dy = jnp.where(in_dom, 0, dy)
        return word >= 2, dy, dz, to_x, same, k

    def accumulator(slot, dx, r):
        live, dy, dz, to_x, same, k = master(slot, dx, r)
        own = slot < 2
        live = jnp.logical_or(own, live)
        dy, dz = jnp.where(own, 0, dy), jnp.where(own, 0, dz)
        to_x, same = jnp.where(own, dx, to_x), jnp.where(own, r, same)
        k = jnp.where(own, slot, k)
        a = jnp.where(to_x == 0, 120, jnp.where(to_x == 2, 0, 32 + 8 * to_x)) + dz * 2
        middle = jnp.where(dz == 4, 16, 72 + 4 * (dz - 3))
        outer = jnp.where(dz < 3, 136 + 8 * dz, 112 + 8 * dz)
        b = jnp.where((dz - 4) * (dz - 4) < 2, middle, outer) + to_x * 2
        c = jnp.where(dy == 2, 24, jnp.where(dy == 1, 88, 104)) + r * 8 + dx * 2
        return live, jnp.where(dy > 0, c, jnp.where(same == 0, a, b)) + k

    def append(tile_ref, tile, block_ref, start, place):
        def into(out, place):
            n = out[0]
            out[0] = n + 1
            for j, value in enumerate((tile_ref, tile, block_ref, start, place)):
                out[1 + ENTRIES * j + n] = value

        for out, begin, size in zip(lists, STARTS, SIZES):

            @pl.when(jnp.logical_and(place >= begin, place < begin + size))
            def _(out=out, begin=begin):
                into(out, place - begin)

    @pl.loop(0, 2 * NT)
    def _(i):
        r, t = i >> 4, i & 15
        live, place = accumulator(row[r * INTS + HS + t], 0, r)

        @pl.when(live)
        def _():
            append(5 + r, t, 0, HEAD + BLK * (2 * r + row[r * INTS + HT + t]), place)

    @pl.loop(0, picked[0])
    def _(i):
        which = picked[1 + i]
        dx, r, t = which >> 5, (which >> 4) & 1, which & 15
        base = (which >> 4) * INTS
        target_live, dy, dz, _, same, k = master(row[base + FT + t], dx, r)
        source_live, place = accumulator(row[base + FS + t], dx, r)

        @pl.when(jnp.logical_and(target_live, source_live))
        def _():
            far = dz == 4
            block_ref = jnp.where(far, 4 + same, jnp.where(dz > 4, dz + 1, dz))
            block_ref = jnp.where(dy > 0, 12 - dy, block_ref)
            j = jnp.where(far, k, 2 * same + k)
            start = jnp.where(jnp.logical_and(far, same == 1), 0, HEAD) + BLK * j
            tile_ref = jnp.where(dx == 2, 3 + r, jnp.where(dx == 3, 2, dx))
            append(tile_ref, jnp.where(dx == 2, t, r * NT + t), block_ref, start, place)


bar = lax.optimization_barrier


def tile_product(tile, block):
    return lax.dot_general(tile, block, (((0,), (0,)), ((), ())), preferred_element_type=f32)


def tile_kernel(parts, todo, *refs):
    tile_refs, block_refs, outs = refs[:7], refs[7:19], refs[19 : 19 + len(parts)]
    acc, tiles, blocks, tile_sems, block_sems, out_sems = refs[19 + len(parts) :]
    n = todo[0]

    def held(c):
        return jnp.clip(n - c * SLOTS, 0, SLOTS)

    def start(c):
        def one(j, _):
            i = c * SLOTS + j
            which, tile = todo[1 + i], todo[1 + ENTRIES + i]
            for s, ref in enumerate(tile_refs):

                @pl.when(which == s)
                def _(ref=ref):
                    pltpu.make_async_copy(ref.at[tile], tiles.at[j], tile_sems.at[j]).start()

            which_block = todo[1 + 2 * ENTRIES + i]
            at = pl.multiple_of(todo[1 + 3 * ENTRIES + i], 16)
            for s, ref in enumerate(block_refs):

                @pl.when(which_block == s)
                def _(ref=ref):
                    copy = pltpu.make_async_copy(ref.at[pl.ds(at, BLK)], blocks.at[j], block_sems.at[j])
                    copy.start()

            return 0

        lax.fori_loop(0, held(c), one, 0)

    def finish(c):
        def one(j, _):
            place = todo[1 + 4 * ENTRIES + c * SLOTS + j]
            pltpu.make_async_copy(tile_refs[0].at[0], tiles.at[j], tile_sems.at[j]).wait()
            pltpu.make_async_copy(block_refs[0].at[pl.ds(0, BLK)], blocks.at[j], block_sems.at[j]).wait()
            term = tile_product(tiles[j], blocks[j])
            acc[place] = (acc[place].astype(f32) + term).astype(bf16)
            return 0

        lax.fori_loop(0, held(c), one, 0)

    start(0)

    @pl.loop(0, acc.shape[0])
    def _(b):
        acc[b] = jnp.zeros((BLK, HALF), bf16)

    def step(c, _):
        finish(c)
        start(c + 1)
        return 0

    lax.fori_loop(0, (n + SLOTS - 1) // SLOTS, step, 0)
    copies = [
        pltpu.make_async_copy(acc.at[pl.ds(s, m)], out, out_sems.at[j])
        for j, ((s, m), out) in enumerate(zip(parts, outs))
    ]
    for copy in copies:
        copy.start()
    for copy in copies:
        copy.wait()


def tile_sums(group, todo, tile_refs, block_refs):
    parts, size = GROUPS[group], SIZES[group]
    return pl.pallas_call(
        lambda *refs: tile_kernel(parts, *refs),
        out_shape=[jax.ShapeDtypeStruct((m, BLK, HALF), bf16) for _, m in parts],
        in_specs=[SMEM] + [ANY] * 19,
        out_specs=[HBM] * len(parts),
        scratch_shapes=[
            pltpu.VMEM((size, BLK, HALF), bf16),
            pltpu.VMEM((SLOTS, BLK, BLK), bf16),
            pltpu.VMEM((SLOTS, BLK, HALF), bf16),
            pltpu.SemaphoreType.DMA((SLOTS,)),
            pltpu.SemaphoreType.DMA((SLOTS,)),
            pltpu.SemaphoreType.DMA((len(parts),)),
        ],
        compiler_params=pltpu.CompilerParams(vmem_limit_bytes=10 * MIB),
        cost_estimate=pl.CostEstimate(flops=10**9, bytes_accessed=2 * 10**7, transcendentals=0),
    )(todo, *tile_refs, *block_refs)


def agg_kernel(meta, pre_act, cotan, w_neigh, grad_pre, agg_own, agg_other):
    grad = jnp.where(pre_act[...] > 0, cotan[...], jnp.zeros_like(cotan))
    grad_pre[...] = grad
    for out, half in ((agg_other, 1 - meta[0]), (agg_own, meta[0])):
        weight = w_neigh[pl.ds(pl.multiple_of(half * HALF, HALF), HALF), :]
        product = lax.dot_general(grad, weight, (((1,), (1,)), ((), ())), preferred_element_type=f32)
        out[...] = product.astype(bf16)


def agg_terms(meta, pre_act, cotan, w_neigh):
    half = jax.ShapeDtypeStruct((HALF, HALF), bf16)
    return pl.pallas_call(
        agg_kernel,
        out_shape=[jax.ShapeDtypeStruct(pre_act.shape, bf16), half, half],
        in_specs=[SMEM] + [VMEM] * 3,
        out_specs=[VMEM] * 3,
        compiler_params=pltpu.CompilerParams(vmem_limit_bytes=6 * MIB),
    )(meta, pre_act, cotan, w_neigh)


def join_kernel(head, own, sib, out):
    out[:HEAD] = head[...]
    out[HEAD : HEAD + HALF] = own[...]
    out[HEAD + HALF :] = sib[...]


def join_chunk(head, own, sib):
    return pl.pallas_call(
        join_kernel,
        out_shape=jax.ShapeDtypeStruct((HEAD + 2 * HALF, HALF), bf16),
        in_specs=[VMEM] * 3,
        out_specs=VMEM,
        compiler_params=pltpu.CompilerParams(vmem_limit_bytes=4 * MIB),
    )(head, own, sib)


def weight_kernel(meta, feats, neigh, grad_pre, mine, other):
    core = meta[0]
    low, high = grad_pre[:, :HALF], grad_pre[:, HALF:]
    for out, from_low in ((mine, core == 0), (other, core == 1)):
        part = jnp.where(from_low, low, high)
        bias = jnp.sum(part.astype(f32), axis=0, keepdims=True)
        for g in range(NY):
            source = feats if g < 2 else neigh
            cols = source[:, (g % 2) * HALF : (g % 2 + 1) * HALF]
            out[g, :, :HALF] = tile_product(cols, part)
            out[g, :, HALF:] = jnp.zeros((HALF, BLK), f32)
            if g == 0:
                out[g, 0:1, HALF:] = bias[:, :BLK]
                out[g, 1:2, HALF:] = bias[:, BLK:]


def weight_terms(meta, feats, neigh, grad_pre):
    return pl.pallas_call(
        weight_kernel,
        out_shape=[jax.ShapeDtypeStruct((NY, HALF, HALF + BLK), f32)] * 2,
        in_specs=[SMEM] + [VMEM] * 3,
        out_specs=[VMEM] * 2,
        compiler_params=pltpu.CompilerParams(vmem_limit_bytes=10 * MIB),
    )(meta, feats, neigh, grad_pre)


def scalars(kernel, sizes, *args, tables=(), scratch=()):
    return pl.pallas_call(
        kernel,
        out_shape=[jax.ShapeDtypeStruct((n,), i32) for n in sizes],
        in_specs=[SMEM] * len(args) + [ANY] * len(tables),
        out_specs=[SMEM] * len(sizes),
        scratch_shapes=scratch,
        compiler_params=pltpu.CompilerParams(vmem_limit_bytes=3 * MIB),
    )(*args, *tables)


def add(*terms):
    total = terms[0].astype(f32)
    for term in terms[1:]:
        total = total + term.astype(f32)
    return total


def add_head(value, head):
    n = head.shape[0]
    return jnp.concatenate([add(value[:n], head).astype(bf16), value[n:].astype(bf16)])


def add_tail(value, tail):
    n = value.shape[0] - tail.shape[0]
    return jnp.concatenate([value[:n].astype(bf16), add(value[n:], tail).astype(bf16)])


def return_sums(first, sums_of):
    a2h, a2t, b4h, b4t, y2h, y2t = first
    b4h, b4t, a2h, a2t, (a1, a3, b3, b5, y1, y3) = sums_of(1, (b4h, b4t, a2h, a2t))
    up, down = shift(b4h, "z", 1), shift(b4t, "z", -1)
    ax_p, ax_m = shift(a2h, "x", 1), shift(a2t, "x", -1)
    up, down, y2h, y2t = bar((up, down, y2h, y2t))
    y_p, y_m = shift(y2h, "group", 1), shift(y2t, "group", -1)

    up, down, ax_p, ax_m, a1, a3, b3, b5 = bar((up, down, ax_p, ax_m, a1, a3, b3, b5))
    up, down, ax_p, ax_m, (a0, b0, b1, b2, b6, b7) = sums_of(2, (up, down, ax_p, ax_m))
    ax_p, ax_m = shift(add_head(a1, ax_p), "x", 1), shift(add_tail(a3, ax_m), "x", -1)
    up, down = shift(add_head(b3, up), "z", 1), shift(add_tail(b5, down), "z", -1)
    up, down, y_p, y_m = bar((up, down, y_p, y_m))
    up, down = add(b2, up).astype(bf16), add(b6, down).astype(bf16)
    up, down = shift(up, "z", 1), shift(down, "z", -1)
    y_p = shift(add_head(y1, y_p), "group", 1)
    y_p, y_m = bar((y_p, y_m))
    y_m = shift(add_tail(y3, y_m), "group", -1)

    def part_a(dz):
        rows = slice(2 * dz, 2 * dz + 2)
        return add(a0[rows], ax_p[rows], ax_m[rows])

    def part_b(dx):
        rows = slice(2 * dx, 2 * dx + 2)
        cross = slice(8 + 2 * dx, 10 + 2 * dx)
        sums = add(b0[rows], up[rows], down[rows], y_p[cross], y_m[cross])
        return jnp.concatenate([sums, add(y_p[rows], y_m[rows])])

    up, down, ax_p, ax_m = bar((up, down, ax_p, ax_m))
    far = part_a(4).astype(bf16)
    up, down = add(b1, up).astype(bf16), add(b7, down).astype(bf16)
    az_p, az_m = shift(far[:1], "z", 1), shift(far[1:], "z", -1)
    up, down = shift(up, "z", 1), shift(down, "z", -1)
    az_p, az_m = add_head(part_a(3), az_p), add_tail(part_a(5), az_m)
    az_p, az_m = shift(az_p, "z", 1), shift(az_m, "z", -1)
    az_p, az_m = add(part_a(2), az_p).astype(bf16), add(part_a(6), az_m).astype(bf16)
    far = part_b(2).astype(bf16)
    az_p, az_m, far = bar((az_p, az_m, far))
    bx_p, bx_m = shift(far[:2], "x", 1), shift(far[2:], "x", -1)
    az_p, az_m = shift(az_p, "z", 1), shift(az_m, "z", -1)
    bx_p, bx_m = add_head(part_b(1), bx_p), add_tail(part_b(3), bx_m)
    az_p, az_m = add(part_a(1), az_p).astype(bf16), add(part_a(7), az_m).astype(bf16)
    az_p, az_m, bx_p, bx_m = bar((az_p, az_m, bx_p, bx_m))
    bx_p, bx_m = shift(bx_p, "x", 1), shift(bx_m, "x", -1)
    az_p, az_m = shift(az_p, "z", 1), shift(az_m, "z", -1)
    sum_b = add(part_b(0), bx_p, bx_m)
    return add(part_a(0), az_p, az_m, sum_b[2:]), sum_b[:2]


def body(
    feats,
    neigh,
    pre_act,
    cotan,
    w_self,
    w_neigh,
    send_list,
    send_live,
    cross_list,
    cross_live,
    home_tiles,
    home_target,
    home_source,
    far_tiles,
    far_target,
    far_source,
    far_count,
):
    y, z, x, core = (lax.axis_index(name) for name in AXES)
    meta = jnp.stack([core, z, x, y]).astype(i32)
    first_core = core == 0
    cols = (((1,), (1,)), ((), ()))
    ints = jnp.concatenate(
        [
            (send_live * 2 + send_list).reshape(-1),
            (cross_live * 2 + cross_list).reshape(-1),
            home_target[0, 0],
            home_source[0, 0],
            far_target[0, 0],
            far_source[0, 0],
            far_count[0],
            jnp.zeros((INTS - FC - 1,), i32),
        ]
    )
    row = jnp.stack([ints, shift(ints, "x", -1), shift(ints, "x", 2), shift(ints, "x", 1)])
    row = jnp.stack([row, shift(row, "core", 1)], axis=1)
    words = row[:, :, :CROSS].reshape(2, HALF).astype(bf16)
    cross_words = jnp.pad(row[:, :, CROSS:HT].reshape(1, BLK // 2).astype(bf16), ((0, 0), (0, HALF - BLK // 2)))
    row = row.reshape(-1)

    def join(mine, other):
        low, high = jnp.where(first_core, mine, other), jnp.where(first_core, other, mine)
        return jnp.concatenate([low, high], axis=-1)

    grad_pre, agg_own, agg_other = agg_terms(meta, pre_act, cotan, w_neigh)
    head = jnp.concatenate([words, cross_words, jnp.zeros((HEAD - 3, HALF), bf16)])
    chunk = join_chunk(head, agg_own, shift(agg_other, "core", 1))

    far_own, home_own = far_tiles[0, 0], home_tiles[0, 0]
    mine, other = weight_terms(meta, feats, neigh, grad_pre)

    far_both = jnp.concatenate([far_own, shift(far_own, "core", 1)])
    home_sib = shift(home_own, "core", 1)
    chunk, far_both, home_sib, mine, other = bar((chunk, far_both, home_sib, mine, other))
    up1, dn1 = shift(chunk, "z", 1), shift(chunk, "z", -1)
    tiles3, tiles1 = shift(far_both, "x", 1), shift(far_both, "x", -1)
    other = shift(other, "core", 1)
    up1, dn1, chunk, row, mine, other = bar((up1, dn1, chunk, row, mine, other))
    weights = (mine + other).reshape(4 * HALF, HALF + BLK)
    weights = lax.psum_scatter(weights, "group", scatter_dimension=0, tiled=True)
    weights = lax.psum_scatter(weights, "z", scatter_dimension=0, tiled=True)
    weights = jnp.pad(weights, ((0, 16), (0, 0)))
    weights = lax.all_gather(weights, ("group", "x"), axis=0).reshape(NY, NX, 48, HALF + BLK)
    weights = jnp.sum(weights[:, :, :32], axis=1)
    weights = lax.all_gather(weights, "z", axis=0)
    up2, dn2 = shift(up1, "z", 1), shift(dn1, "z", -1)
    y1 = shift(chunk, "group", 1)
    (picked,) = scalars(pick_kernel, (PICKED,), meta, row)
    up2, dn2, y1, tiles1, tiles3, chunk, picked = bar((up2, dn2, y1, tiles1, tiles3, chunk, picked))
    up3, dn3 = shift(up2, "z", 1), shift(dn2, "z", -1)
    tiles2h, tiles2t = shift(tiles3[:NT], "x", 1), shift(tiles1[NT:], "x", -1)
    y3 = shift(chunk, "group", 3)
    up3, dn3, y3, chunk = bar((up3, dn3, y3, chunk))
    middle = HEAD + 2 * BLK
    up4, dn4 = shift(up3[:middle], "z", 1), shift(dn3[middle:], "z", -1)
    y2 = shift(chunk, "group", 2)
    up4, dn4, tiles2h, tiles2t, y2 = bar((up4, dn4, tiles2h, tiles2t, y2))

    tile_refs = [far_both, tiles1, tiles3, tiles2h, tiles2t, home_own, home_sib]
    block_refs = [chunk, dn1, dn2, dn3, up4, dn4, up3, up2, up1, y1, y2, y3]
    heads = [chunk, dn1, dn2, dn3, up4, up3, up2, up1, y1, y2, y3]
    todo = scalars(
        list_kernel,
        (LIST,) * 3,
        meta,
        row,
        picked,
        tables=heads,
        scratch=[
            pltpu.VMEM((len(heads), HEAD, HALF), bf16),
            pltpu.VMEM((len(heads), HEAD, HALF), i32),
            pltpu.SMEM((len(heads), 8, HALF), i32),
            pltpu.SemaphoreType.DMA((len(heads),)),
        ],
    )

    def sums_of(group, arrived):
        *arrived, now = bar((*arrived, todo[group]))
        return *arrived, tile_sums(group, now, tile_refs, block_refs)

    (first,) = sums_of(0, ())
    sum_a, sum_b = return_sums(first, sums_of)
    self_grad = lax.dot_general(grad_pre, w_self, cols, preferred_element_type=f32)
    weights, sum_b = bar((weights, sum_b))
    other = shift(sum_b, "core", 1)
    weights_sib = shift(weights, "core", 1)

    def rows_of(value):
        return value.transpose(1, 0, 2, 3).reshape(4 * HALF, HALF + BLK)

    weights, weights_sib = rows_of(weights), rows_of(weights_sib)
    sums = join(weights[:, :HALF], weights_sib[:, :HALF])
    bias = join(weights[:2, HALF:].reshape(-1), weights_sib[:2, HALF:].reshape(-1))
    grad_input = self_grad + join(sum_a.reshape(2 * BLK, HALF), other.reshape(2 * BLK, HALF))
    return grad_input.astype(bf16), sums[:512], sums[512:], bias


def solution(mesh):
    fine = Mesh(mesh.devices.reshape(NY, NZ, NX, 2), AXES)
    rows = P(AXES, None)
    part = lambda extra: P("group", DOM, *([None] * extra))
    return jax.shard_map(
        body,
        mesh=fine,
        in_specs=(rows,) * 4
        + (P(), P())
        + (part(1), part(1), part(2), part(2), part(3), part(1), part(1), part(3), part(1), part(1), part(0)),
        out_specs=(rows, P(), P(), P()),
        check_vma=False,
    )
```

profile of v0, /device:TPU:16, one launch (start us, length us, event | category | flops | bytes accessed | tf_op | source)
XLA Modules:
  0.0 304.9 jit_solution(13818785399428226027)
XLA Ops:
  11.8 2.7 collective-permute-start.1
  30.0 2.7 collective-permute-start.13
  32.7 1.9 collective-permute-start.7
  34.6 3.9 %collective-permute-start.8 = (bf16[528,256]{1,0:T(8,128)(2,1)S(1)}, bf16[528,256]{1,0:T(8,128)(2,1)S(1)}, u32[]{:S(2)}, u32[]{:S(2)}) collective-permute-start(bf16[528,256]{1,0:T(8,128)(2,1)S(1)} %shard_map.193.refs_0_.refs_8_), channel_id=1, source_target_pairs={{0,56},{8,0},{16,8},{24,16},{32,24},{40,32},{48,40},{56,48},{1,57}... | collective-permute-start | bytes 811016 | tf_op jit(solution)/shard_map/ppermute | solution.py:39
  38.6 6.8 %collective-permute-done.7.refs_7_.refs_16_ = bf16[528,256]{1,0:T(8,128)(2,1)S(1)} collective-permute-done((bf16[528,256]{1,0:T(8,128)(2,1)S(1)}, bf16[528,256]{1,0:T(8,128)(2,1)S(1)}, u32[]{:S(2)}, u32[]{:S(2)}) %collective-permute-start.7) | collective-permute-done | bytes 270368 | tf_op jit(solution)/shard_map/ppermute | solution.py:39
  48.3 3.2 %collective-permute-start.11 = (bf16[528,256]{1,0:T(8,128)(2,1)}, bf16[528,256]{1,0:T(8,128)(2,1)S(1)}, u32[]{:S(2)}, u32[]{:S(2)}) collective-permute-start(bf16[528,256]{1,0:T(8,128)(2,1)} %copy-done.4), channel_id=1, source_target_pairs={{0,56},{8,0},{16,8},{24,16},{32,24},{40,32},{48,40},{56,48},{1,57}... | collective-permute-start | bytes 811016 | tf_op jit(solution)/shard_map/ppermute | solution.py:39
  52.8 2.1 shard_map.195.picked
  55.7 3.5 %collective-permute-done.14.refs_3_ = bf16[32,128,128]{2,1,0:T(8,128)(2,1)} collective-permute-done((bf16[32,128,128]{2,1,0:T(8,128)(2,1)S(1)}, bf16[32,128,128]{2,1,0:T(8,128)(2,1)}, u32[]{:S(2)}, u32[]{:S(2)}) %collective-permute-start.14) | collective-permute-done | bytes 1048608 | tf_op jit(solution)/shard_map/ppermute | solution.py:39
  59.2 2.3 collective-permute-start.15
  61.5 4.0 %collective-permute-start.16 = (bf16[528,256]{1,0:T(8,128)(2,1)S(1)}, bf16[528,256]{1,0:T(8,128)(2,1)S(1)}, u32[]{:S(2)}, u32[]{:S(2)}) collective-permute-start(bf16[528,256]{1,0:T(8,128)(2,1)S(1)} %collective-permute-done.11.refs_2_.refs_10_), channel_id=1, source_target_pairs={{0,56},{8,0},{16,8},{24,16},{32,24},{40,32},{48,40},{56,48},{1,57}... | collective-permute-start | bytes 811016 | tf_op jit(solution)/shard_map/ppermute | solution.py:39
  67.2 3.3 %collective-permute-start.21 = (bf16[16,128,128]{2,1,0:T(8,128)(2,1)S(1)}, bf16[16,128,128]{2,1,0:T(8,128)(2,1)S(1)}, u32[]{:S(2)}, u32[]{:S(2)}) collective-permute-start(bf16[16,128,128]{2,1,0:T(8,128)(2,1)S(1)} %slice.270), channel_id=1, source_target_pairs={{0,6},{2,0},{4,2},{6,4},{1,7},{3,1},{5,3},{7,5},{8,14},{10,8},{12,... | collective-permute-start | bytes 1572872 | tf_op jit(solution)/shard_map/ppermute | solution.py:39
  71.4 7.9 %collective-permute-done.17.refs_10_.refs_19_ = bf16[528,256]{1,0:T(8,128)(2,1)S(1)} collective-permute-done((bf16[528,256]{1,0:T(8,128)(2,1)S(1)}, bf16[528,256]{1,0:T(8,128)(2,1)S(1)}, u32[]{:S(2)}, u32[]{:S(2)}) %collective-permute-start.17) | collective-permute-done | bytes 270368 | tf_op jit(solution)/shard_map/ppermute | solution.py:39
  80.2 3.3 %collective-permute-start.19 = (bf16[256,256]{1,0:T(8,128)(2,1)S(1)}, bf16[256,256]{1,0:T(8,128)(2,1)S(1)}, u32[]{:S(2)}, u32[]{:S(2)}) collective-permute-start(bf16[256,256]{1,0:T(8,128)(2,1)S(1)} %slice.268), channel_id=1, source_target_pairs={{0,56},{8,0},{16,8},{24,16},{32,24},{40,32},{48,40},{56,48},{1,57}... | collective-permute-start | bytes 393224 | tf_op jit(solution)/shard_map/ppermute | solution.py:39
  83.5 2.5 collective-permute-done.19.refs_13_
  86.5 1.9 collective-permute-done.22.refs_9_.refs_18_
  88.4 7.6 %shard_map.196 = (s32[801]{0:T(1024)S(1)}, s32[801]{0:T(1024)S(1)}, s32[801]{0:T(1024)S(1)}) custom-call(s32[4]{0:T(128)S(1)} %pad_add_fusion.2.meta, s32[2048]{0:T(1024)S(1)} %bitcast.43, s32[129]{0:T(256)S(1)} %shard_map.195.picked, bf16[528,256]{1,0:T(8,128)(2,1)S(1)} %shard_map.193.refs_0_.refs_8_, bf16[528,256]{1,0:T(8,128)(2,1)S(1)} %copy-done.5, ...), custom_call_target="tpu_custom_call" | custom-call | tf_op jit(solution)/shard_map/pallas_call | solution.py:307
  96.0 5.2 %shard_map.197 = (bf16[8,128,256]{2,1,0:T(8,128)(2,1)S(1)}, bf16[8,128,256]{2,1,0:T(8,128)(2,1)S(1)}, bf16[4,128,256]{2,1,0:T(8,128)(2,1)S(1)}, bf16[4,128,256]{...) custom-call(s32[801]{0:T(1024)S(1)} %get-tuple-element.124.refs_0_, ...), custom_call_target="tpu_custom_call" | custom-call | flops 1000000000 | bytes 20000000 | tf_op jit(solution)/shard_map/pallas_call | solution.py:226
  101.3 3.2 %collective-permute-start.26 = (bf16[8,128,256]{2,1,0:T(8,128)(2,1)S(1)}, bf16[8,128,256]{2,1,0:T(8,128)(2,1)S(1)}, u32[]{:S(2)}, u32[]{:S(2)}) collective-permute-start(bf16[8,128,256]{2,1,0:T(8,128)(2,1)S(1)} %get-tuple-element.141), channel_id=1, source_target_pairs={{0,6},{2,0},{4,2},{6,4},{1,7},{3,1},{5,3},{7,5},{8,14},{10,8},{12,... | collective-permute-start | bytes 1572872 | tf_op jit(solution)/shard_map/ppermute | solution.py:39
  104.5 3.2 %collective-permute-start.24 = (bf16[4,128,256]{2,1,0:T(8,128)(2,1)S(1)}, bf16[4,128,256]{2,1,0:T(8,128)(2,1)S(1)}, u32[]{:S(2)}, u32[]{:S(2)}) collective-permute-start(bf16[4,128,256]{2,1,0:T(8,128)(2,1)S(1)} %get-tuple-element.135), channel_id=1, source_target_pairs={{0,56},{8,0},{16,8},{24,16},{32,24},{40,32},{48,40},{56,48},{1,57}... | collective-permute-start | bytes 786440 | tf_op jit(solution)/shard_map/ppermute | solution.py:39
  107.8 6.8 %shard_map.198 = (bf16[16,128,256]{2,1,0:T(8,128)(2,1)S(1)}, bf16[16,128,256]{2,1,0:T(8,128)(2,1)S(1)}, bf16[8,128,256]{2,1,0:T(8,128)(2,1)S(1)}, bf16[8,128,256...) custom-call(s32[801]{0:T(1024)S(1)} %get-tuple-element.142.refs_0_, ...), custom_call_target="tpu_custom_call" | custom-call | flops 1000000000 | bytes 20000000 | tf_op jit(solution)/shard_map/pallas_call | solution.py:226
  115.5 5.9 %collective-permute-start.29 = (bf16[8,128,256]{2,1,0:T(8,128)(2,1)}, bf16[8,128,256]{2,1,0:T(8,128)(2,1)}, u32[]{:S(2)}, u32[]{:S(2)}) collective-permute-start(bf16[8,128,256]{2,1,0:T(8,128)(2,1)} %get-tuple-element.159), channel_id=1, source_target_pairs={{0,64},{64,128},{128,192},{192,0},{1,65},{65,129},{129,193},{193,1... | collective-permute-start | bytes 1572872 | tf_op jit(solution)/shard_map/ppermute | solution.py:39
  122.4 8.7 %collective-permute-start.27 = (bf16[8,128,256]{2,1,0:T(8,128)(2,1)}, bf16[8,128,256]{2,1,0:T(8,128)(2,1)}, u32[]{:S(2)}, u32[]{:S(2)}) collective-permute-start(bf16[8,128,256]{2,1,0:T(8,128)(2,1)} %pad_maximum_fusion.6), channel_id=1, source_target_pairs={{0,8},{8,16},{16,24},{24,32},{32,40},{40,48},{48,56},{56,0},{1,9},... | collective-permute-start | bytes 1572872 | tf_op jit(solution)/shard_map/ppermute | solution.py:39
  132.1 3.2 %collective-permute-start.28 = (bf16[8,128,256]{2,1,0:T(8,128)(2,1)}, bf16[8,128,256]{2,1,0:T(8,128)(2,1)}, u32[]{:S(2)}, u32[]{:S(2)}) collective-permute-start(bf16[8,128,256]{2,1,0:T(8,128)(2,1)} %pad_maximum_fusion.7), channel_id=1, source_target_pairs={{0,56},{8,0},{16,8},{24,16},{32,24},{40,32},{48,40},{56,48},{1,57}... | collective-permute-start | bytes 1572872 | tf_op jit(solution)/shard_map/ppermute | solution.py:39
  137.4 11.3 %shard_map.199 = (bf16[16,128,256]{2,1,0:T(8,128)(2,1)S(1)}, bf16[8,128,256]{2,1,0:T(8,128)(2,1)S(1)}, bf16[8,128,256]{2,1,0:T(8,128)(2,1)S(1)}, bf16[8,128,256]...) custom-call(s32[801]{0:T(1024)S(1)} %get-tuple-element.152.refs_0_, ...), custom_call_target="tpu_custom_call" | custom-call | flops 1000000000 | bytes 20000000 | tf_op jit(solution)/shard_map/pallas_call | solution.py:226
  156.1 2.1 add_convert_fusion.7
  158.2 2.1 add_convert_fusion.6
  160.3 3.1 %collective-permute-start.32 = (bf16[8,128,256]{2,1,0:T(8,128)(2,1)}, bf16[8,128,256]{2,1,0:T(8,128)(2,1)}, u32[]{:S(2)}, u32[]{:S(2)}) collective-permute-start(bf16[8,128,256]{2,1,0:T(8,128)(2,1)} %add_convert_fusion.6), channel_id=1, source_target_pairs={{0,56},{8,0},{16,8},{24,16},{32,24},{40,32},{48,40},{56,48},{1,57}... | collective-permute-start | bytes 1572872 | tf_op jit(solution)/shard_map/ppermute | solution.py:39
  165.1 25.0 %reduce-scatter.5.cloned.1.call-done = f32[32,384]{1,0:T(8,128)} async-done(((f32[256,384]{1,0:T(8,128)}), f32[32,384]{1,0:T(8,128)}) %reduce-scatter.5.cloned.1.call-update) | async-done | bytes 49168 | tf_op jit(solution)/shard_map/reduce_scatter | solution.py:445
  194.5 2.0 add_convert_fusion.2
  200.3 2.1 add_convert_fusion.3
  204.5 4.5 %collective-permute-done.37 = bf16[1,128,256]{2,1,0:T(8,128)(2,1)S(1)} collective-permute-done((bf16[1,128,256]{2,1,0:T(8,128)(2,1)S(1)}, bf16[1,128,256]{2,1,0:T(8,128)(2,1)S(1)}, u32[]{:S(2)}, u32[]{:S(2)}) %collective-permute-start.37) | collective-permute-done | bytes 65568 | tf_op jit(solution)/shard_map/ppermute | solution.py:39
  209.0 2.4 collective-permute-start.38
  211.4 3.8 %collective-permute-done.41 = bf16[16,128,256]{2,1,0:T(8,128)(2,1)S(1)} collective-permute-done((bf16[16,128,256]{2,1,0:T(8,128)(2,1)S(1)}, bf16[16,128,256]{2,1,0:T(8,128)(2,1)S(1)}, u32[]{:S(2)}, u32[]{:S(2)}) %collective-permute-start.41) | collective-permute-done | bytes 1048608 | tf_op jit(solution)/shard_map/ppermute | solution.py:39
  219.6 20.3 %all-gather.5.cloned.1.call-done = f32[768,384]{1,0:T(8,128)} async-done(((f32[48,384]{1,0:T(8,128)}), f32[768,384]{1,0:T(8,128)}) %all-gather.5.cloned.1.call-update) | async-done | bytes 1179664 | tf_op jit(solution)/shard_map/all_gather | solution.py:447
  239.9 1.9 slice_reduce_fusion
  244.1 4.8 %collective-permute-done.36 = bf16[2,128,256]{2,1,0:T(8,128)(2,1)S(1)} collective-permute-done((bf16[2,128,256]{2,1,0:T(8,128)(2,1)S(1)}, bf16[2,128,256]{2,1,0:T(8,128)(2,1)S(1)}, u32[]{:S(2)}, u32[]{:S(2)}) %collective-permute-start.36) | collective-permute-done | bytes 131104 | tf_op jit(solution)/shard_map/ppermute | solution.py:39
  252.6 2.0 collective-permute-start.44
  254.6 2.2 collective-permute-start.46
  257.7 1.6 add_convert_fusion.11
  262.7 2.7 collective-permute-start.50
  265.4 3.9 %collective-permute-done.50 = bf16[4,128,256]{2,1,0:T(8,128)(2,1)S(1)} collective-permute-done((bf16[4,128,256]{2,1,0:T(8,128)(2,1)S(1)}, bf16[4,128,256]{2,1,0:T(8,128)(2,1)S(1)}, u32[]{:S(2)}, u32[]{:S(2)}) %collective-permute-start.50) | collective-permute-done | bytes 262176 | tf_op jit(solution)/shard_map/ppermute | solution.py:39
  269.3 3.7 %collective-permute-done.49 = bf16[4,128,256]{2,1,0:T(8,128)(2,1)S(1)} collective-permute-done((bf16[4,128,256]{2,1,0:T(8,128)(2,1)S(1)}, bf16[4,128,256]{2,1,0:T(8,128)(2,1)S(1)}, u32[]{:S(2)}, u32[]{:S(2)}) %collective-permute-start.49) | collective-permute-done | bytes 262176 | tf_op jit(solution)/shard_map/ppermute | solution.py:39
  273.1 9.6 %all-gather.7.cloned.1.call-done = f32[32,32,384]{2,1,0:T(8,128)} async-done(((f32[4,32,384]{2,1,0:T(8,128)}), f32[32,32,384]{2,1,0:T(8,128)}) %all-gather.7.cloned.1.call-update) | async-done | bytes 1572880 | tf_op jit(solution)/shard_map/all_gather | solution.py:449
  283.2 2.6 collective-permute-start.48
  285.8 1.5 copy.31
  288.7 3.4 %collective-permute-done.47 = bf16[2,128,256]{2,1,0:T(8,128)(2,1)S(1)} collective-permute-done((bf16[2,128,256]{2,1,0:T(8,128)(2,1)S(1)}, bf16[2,128,256]{2,1,0:T(8,128)(2,1)S(1)}, u32[]{:S(2)}, u32[]{:S(2)}) %collective-permute-start.47) | collective-permute-done | bytes 131104 | tf_op jit(solution)/shard_map/ppermute | solution.py:39
  294.3 1.5 copy.32
  296.0 1.6 pad_maximum_fusion
  (229 shorter events, 71.8 us)
Async XLA Ops:
  7.2 146.7 %reduce-scatter.3.cloned.1.call-start = ((), (), s32[]{:S(2)}) async-start(), calls=%async_computation.2 | async-start | bytes 1966080 | tf_op jit(solution)/shard_map/reduce_scatter | solution.py:444
  15.9 12.5 %collective-permute-start.5 = (bf16[16,128,128]{2,1,0:T(8,128)(2,1)}, bf16[16,128,128]{2,1,0:T(8,128)(2,1)}, u32[]{:S(2)}, u32[]{:S(2)}) collective-permute-start(bf16[16,128,128]{2,1,0:T(8,128)(2,1)} %bitcast.54), channel_id=1, source_target_pairs={{0,1},{1,0},{2,3},{3,2},{4,5},{5,4},{6,7},{7,6},{8,9},{9,8},{10,11... | collective-permute-start | bytes 1572872 | tf_op jit(solution)/shard_map/ppermute | solution.py:39
  15.9 13.9 %collective-permute-start.6 = (bf16[16,128,128]{2,1,0:T(8,128)(2,1)}, bf16[16,128,128]{2,1,0:T(8,128)(2,1)S(1)}, u32[]{:S(2)}, u32[]{:S(2)}) collective-permute-start(bf16[16,128,128]{2,1,0:T(8,128)(2,1)} %bitcast.38), channel_id=1, source_target_pairs={{0,1},{1,0},{2,3},{3,2},{4,5},{5,4},{6,7},{7,6},{8,9},{9,8},{10,11... | collective-permute-start | bytes 1572872 | tf_op jit(solution)/shard_map/ppermute | solution.py:39
  18.1 10.0 %collective-permute-start.3 = (s32[4,256]{1,0:T(4,128)S(1)}, s32[4,256]{1,0:T(4,128)S(1)}, u32[]{:S(2)}, u32[]{:S(2)}) collective-permute-start(s32[4,256]{1,0:T(4,128)S(1)} %get-tuple-element.221), channel_id=1, source_target_pairs={{0,1},{1,0},{2,3},{3,2},{4,5},{5,4},{6,7},{7,6},{8,9},{9,8},{10,11... | collective-permute-start | bytes 12296 | tf_op jit(solution)/shard_map/ppermute | solution.py:39
  29.9 16.2 %collective-permute-start.9 = (f32[4,256,384]{2,1,0:T(8,128)}, f32[4,256,384]{2,1,0:T(8,128)S(1)}, u32[]{:S(2)}, u32[]{:S(2)}) collective-permute-start(f32[4,256,384]{2,1,0:T(8,128)} %copy-done.31), channel_id=1, source_target_pairs={{0,1},{1,0},{2,3},{3,2},{4,5},{5,4},{6,7},{7,6},{8,9},{9,8},{10,11... | collective-permute-start | bytes 4718600 | tf_op jit(solution)/shard_map/ppermute | solution.py:39
  30.0 25.7 %collective-permute-start.13 = (bf16[32,128,128]{2,1,0:T(8,128)(2,1)S(1)}, bf16[32,128,128]{2,1,0:T(8,128)(2,1)S(1)}, u32[]{:S(2)}, u32[]{:S(2)}) collective-permute-start(bf16[32,128,128]{2,1,0:T(8,128)(2,1)S(1)} %pad_maximum_fusion.1.refs_1_), channel_id=1, source_target_pairs={{0,6},{2,0},{4,2},{6,4},{1,7},{3,1},{5,3},{7,5},{8,14},{10,8},{12,... | collective-permute-start | bytes 3145736 | tf_op jit(solution)/shard_map/ppermute | solution.py:39
  32.7 26.5 %collective-permute-start.14 = (bf16[32,128,128]{2,1,0:T(8,128)(2,1)S(1)}, bf16[32,128,128]{2,1,0:T(8,128)(2,1)}, u32[]{:S(2)}, u32[]{:S(2)}) collective-permute-start(bf16[32,128,128]{2,1,0:T(8,128)(2,1)S(1)} %pad_maximum_fusion.1.refs_1_), channel_id=1, source_target_pairs={{0,2},{2,4},{4,6},{6,0},{1,3},{3,5},{5,7},{7,1},{8,10},{10,12},{12... | collective-permute-start | bytes 3145736 | tf_op jit(solution)/shard_map/ppermute | solution.py:39
  32.7 12.7 %collective-permute-start.7 = (bf16[528,256]{1,0:T(8,128)(2,1)S(1)}, bf16[528,256]{1,0:T(8,128)(2,1)S(1)}, u32[]{:S(2)}, u32[]{:S(2)}) collective-permute-start(bf16[528,256]{1,0:T(8,128)(2,1)S(1)} %shard_map.193.refs_0_.refs_8_), channel_id=1, source_target_pairs={{0,8},{8,16},{16,24},{24,32},{32,40},{40,48},{48,56},{56,0},{1,9},... | collective-permute-start | bytes 811016 | tf_op jit(solution)/shard_map/ppermute | solution.py:39
  34.6 10.7 %collective-permute-start.8 = (bf16[528,256]{1,0:T(8,128)(2,1)S(1)}, bf16[528,256]{1,0:T(8,128)(2,1)S(1)}, u32[]{:S(2)}, u32[]{:S(2)}) collective-permute-start(bf16[528,256]{1,0:T(8,128)(2,1)S(1)} %shard_map.193.refs_0_.refs_8_), channel_id=1, source_target_pairs={{0,56},{8,0},{16,8},{24,16},{32,24},{40,32},{48,40},{56,48},{1,57}... | collective-permute-start | bytes 811016 | tf_op jit(solution)/shard_map/ppermute | solution.py:39
  48.2 141.9 %reduce-scatter.5.cloned.1.call-start = ((), (), s32[]{:S(2)}) async-start(), calls=%async_computation.3 | async-start | bytes 442368 | tf_op jit(solution)/shard_map/reduce_scatter | solution.py:445
  48.2 11.0 %collective-permute-start.10 = (bf16[528,256]{1,0:T(8,128)(2,1)}, bf16[528,256]{1,0:T(8,128)(2,1)S(1)}, u32[]{:S(2)}, u32[]{:S(2)}) collective-permute-start(bf16[528,256]{1,0:T(8,128)(2,1)} %copy-done.2), channel_id=1, source_target_pairs={{0,8},{8,16},{16,24},{24,32},{32,40},{40,48},{48,56},{56,0},{1,9},... | collective-permute-start | bytes 811016 | tf_op jit(solution)/shard_map/ppermute | solution.py:39
  48.3 10.9 %collective-permute-start.11 = (bf16[528,256]{1,0:T(8,128)(2,1)}, bf16[528,256]{1,0:T(8,128)(2,1)S(1)}, u32[]{:S(2)}, u32[]{:S(2)}) collective-permute-start(bf16[528,256]{1,0:T(8,128)(2,1)} %copy-done.4), channel_id=1, source_target_pairs={{0,56},{8,0},{16,8},{24,16},{32,24},{40,32},{48,40},{56,48},{1,57}... | collective-permute-start | bytes 811016 | tf_op jit(solution)/shard_map/ppermute | solution.py:39
  51.6 7.7 %collective-permute-start.12 = (bf16[528,256]{1,0:T(8,128)(2,1)S(1)}, bf16[528,256]{1,0:T(8,128)(2,1)S(1)}, u32[]{:S(2)}, u32[]{:S(2)}) collective-permute-start(bf16[528,256]{1,0:T(8,128)(2,1)S(1)} %shard_map.193.refs_0_.refs_8_), channel_id=1, source_target_pairs={{0,64},{64,128},{128,192},{192,0},{1,65},{65,129},{129,193},{193,1... | collective-permute-start | bytes 811016 | tf_op jit(solution)/shard_map/ppermute | solution.py:39
  59.2 12.2 %collective-permute-start.15 = (bf16[528,256]{1,0:T(8,128)(2,1)S(1)}, bf16[528,256]{1,0:T(8,128)(2,1)S(1)}, u32[]{:S(2)}, u32[]{:S(2)}) collective-permute-start(bf16[528,256]{1,0:T(8,128)(2,1)S(1)} %collective-permute-done.10.refs_6_.refs_15_), channel_id=1, source_target_pairs={{0,8},{8,16},{16,24},{24,32},{32,40},{40,48},{48,56},{56,0},{1,9},... | collective-permute-start | bytes 811016 | tf_op jit(solution)/shard_map/ppermute | solution.py:39
  61.5 9.9 %collective-permute-start.16 = (bf16[528,256]{1,0:T(8,128)(2,1)S(1)}, bf16[528,256]{1,0:T(8,128)(2,1)S(1)}, u32[]{:S(2)}, u32[]{:S(2)}) collective-permute-start(bf16[528,256]{1,0:T(8,128)(2,1)S(1)} %collective-permute-done.11.refs_2_.refs_10_), channel_id=1, source_target_pairs={{0,56},{8,0},{16,8},{24,16},{32,24},{40,32},{48,40},{56,48},{1,57}... | collective-permute-start | bytes 811016 | tf_op jit(solution)/shard_map/ppermute | solution.py:39
  65.5 13.8 %collective-permute-start.17 = (bf16[528,256]{1,0:T(8,128)(2,1)S(1)}, bf16[528,256]{1,0:T(8,128)(2,1)S(1)}, u32[]{:S(2)}, u32[]{:S(2)}) collective-permute-start(bf16[528,256]{1,0:T(8,128)(2,1)S(1)} %shard_map.193.refs_0_.refs_8_), channel_id=1, source_target_pairs={{0,192},{64,0},{128,64},{192,128},{1,193},{65,1},{129,65},{193,129... | collective-permute-start | bytes 811016 | tf_op jit(solution)/shard_map/ppermute | solution.py:39
  67.1 19.4 %collective-permute-start.20 = (bf16[16,128,128]{2,1,0:T(8,128)(2,1)S(1)}, bf16[16,128,128]{2,1,0:T(8,128)(2,1)S(1)}, u32[]{:S(2)}, u32[]{:S(2)}) collective-permute-start(bf16[16,128,128]{2,1,0:T(8,128)(2,1)S(1)} %slice.269), channel_id=1, source_target_pairs={{0,2},{2,4},{4,6},{6,0},{1,3},{3,5},{5,7},{7,1},{8,10},{10,12},{12... | collective-permute-start | bytes 1572872 | tf_op jit(solution)/shard_map/ppermute | solution.py:39
  67.2 19.3 %collective-permute-start.21 = (bf16[16,128,128]{2,1,0:T(8,128)(2,1)S(1)}, bf16[16,128,128]{2,1,0:T(8,128)(2,1)S(1)}, u32[]{:S(2)}, u32[]{:S(2)}) collective-permute-start(bf16[16,128,128]{2,1,0:T(8,128)(2,1)S(1)} %slice.270), channel_id=1, source_target_pairs={{0,6},{2,0},{4,2},{6,4},{1,7},{3,1},{5,3},{7,5},{8,14},{10,8},{12,... | collective-permute-start | bytes 1572872 | tf_op jit(solution)/shard_map/ppermute | solution.py:39
  79.3 9.0 %collective-permute-start.22 = (bf16[528,256]{1,0:T(8,128)(2,1)S(1)}, bf16[528,256]{1,0:T(8,128)(2,1)S(1)}, u32[]{:S(2)}, u32[]{:S(2)}) collective-permute-start(bf16[528,256]{1,0:T(8,128)(2,1)S(1)} %shard_map.193.refs_0_.refs_8_), channel_id=1, source_target_pairs={{0,128},{64,192},{128,0},{192,64},{1,129},{65,193},{129,1},{193,65... | collective-permute-start | bytes 811016 | tf_op jit(solution)/shard_map/ppermute | solution.py:39
  80.1 6.3 %collective-permute-start.18 = (bf16[272,256]{1,0:T(8,128)(2,1)S(1)}, bf16[272,256]{1,0:T(8,128)(2,1)S(1)}, u32[]{:S(2)}, u32[]{:S(2)}) collective-permute-start(bf16[272,256]{1,0:T(8,128)(2,1)S(1)} %slice.267), channel_id=1, source_target_pairs={{0,8},{8,16},{16,24},{24,32},{32,40},{40,48},{48,56},{56,0},{1,9},... | collective-permute-start | bytes 417800 | tf_op jit(solution)/shard_map/ppermute | solution.py:39
  101.2 20.3 %collective-permute-start.25 = (bf16[8,128,256]{2,1,0:T(8,128)(2,1)S(1)}, bf16[8,128,256]{2,1,0:T(8,128)(2,1)S(1)}, u32[]{:S(2)}, u32[]{:S(2)}) collective-permute-start(bf16[8,128,256]{2,1,0:T(8,128)(2,1)S(1)} %get-tuple-element.140), channel_id=1, source_target_pairs={{0,2},{2,4},{4,6},{6,0},{1,3},{3,5},{5,7},{7,1},{8,10},{10,12},{12... | collective-permute-start | bytes 1572872 | tf_op jit(solution)/shard_map/ppermute | solution.py:39
  101.3 20.2 %collective-permute-start.26 = (bf16[8,128,256]{2,1,0:T(8,128)(2,1)S(1)}, bf16[8,128,256]{2,1,0:T(8,128)(2,1)S(1)}, u32[]{:S(2)}, u32[]{:S(2)}) collective-permute-start(bf16[8,128,256]{2,1,0:T(8,128)(2,1)S(1)} %get-tuple-element.141), channel_id=1, source_target_pairs={{0,6},{2,0},{4,2},{6,4},{1,7},{3,1},{5,3},{7,5},{8,14},{10,8},{12,... | collective-permute-start | bytes 1572872 | tf_op jit(solution)/shard_map/ppermute | solution.py:39
  104.5 11.0 %collective-permute-start.23 = (bf16[4,128,256]{2,1,0:T(8,128)(2,1)S(1)}, bf16[4,128,256]{2,1,0:T(8,128)(2,1)S(1)}, u32[]{:S(2)}, u32[]{:S(2)}) collective-permute-start(bf16[4,128,256]{2,1,0:T(8,128)(2,1)S(1)} %get-tuple-element.134), channel_id=1, source_target_pairs={{0,8},{8,16},{16,24},{24,32},{32,40},{40,48},{48,56},{56,0},{1,9},... | collective-permute-start | bytes 786440 | tf_op jit(solution)/shard_map/ppermute | solution.py:39
  104.5 11.0 %collective-permute-start.24 = (bf16[4,128,256]{2,1,0:T(8,128)(2,1)S(1)}, bf16[4,128,256]{2,1,0:T(8,128)(2,1)S(1)}, u32[]{:S(2)}, u32[]{:S(2)}) collective-permute-start(bf16[4,128,256]{2,1,0:T(8,128)(2,1)S(1)} %get-tuple-element.135), channel_id=1, source_target_pairs={{0,56},{8,0},{16,8},{24,16},{32,24},{40,32},{48,40},{56,48},{1,57}... | collective-permute-start | bytes 786440 | tf_op jit(solution)/shard_map/ppermute | solution.py:39
  115.5 40.3 %collective-permute-start.29 = (bf16[8,128,256]{2,1,0:T(8,128)(2,1)}, bf16[8,128,256]{2,1,0:T(8,128)(2,1)}, u32[]{:S(2)}, u32[]{:S(2)}) collective-permute-start(bf16[8,128,256]{2,1,0:T(8,128)(2,1)} %get-tuple-element.159), channel_id=1, source_target_pairs={{0,64},{64,128},{128,192},{192,0},{1,65},{65,129},{129,193},{193,1... | collective-permute-start | bytes 1572872 | tf_op jit(solution)/shard_map/ppermute | solution.py:39
  121.4 34.7 %collective-permute-start.30 = (bf16[8,128,256]{2,1,0:T(8,128)(2,1)}, bf16[8,128,256]{2,1,0:T(8,128)(2,1)}, u32[]{:S(2)}, u32[]{:S(2)}) collective-permute-start(bf16[8,128,256]{2,1,0:T(8,128)(2,1)} %get-tuple-element.160), channel_id=1, source_target_pairs={{0,192},{64,0},{128,64},{192,128},{1,193},{65,1},{129,65},{193,129... | collective-permute-start | bytes 1572872 | tf_op jit(solution)/shard_map/ppermute | solution.py:39
  122.4 33.7 %collective-permute-start.27 = (bf16[8,128,256]{2,1,0:T(8,128)(2,1)}, bf16[8,128,256]{2,1,0:T(8,128)(2,1)}, u32[]{:S(2)}, u32[]{:S(2)}) collective-permute-start(bf16[8,128,256]{2,1,0:T(8,128)(2,1)} %pad_maximum_fusion.6), channel_id=1, source_target_pairs={{0,8},{8,16},{16,24},{24,32},{32,40},{40,48},{48,56},{56,0},{1,9},... | collective-permute-start | bytes 1572872 | tf_op jit(solution)/shard_map/ppermute | solution.py:39
  132.1 24.0 %collective-permute-start.28 = (bf16[8,128,256]{2,1,0:T(8,128)(2,1)}, bf16[8,128,256]{2,1,0:T(8,128)(2,1)}, u32[]{:S(2)}, u32[]{:S(2)}) collective-permute-start(bf16[8,128,256]{2,1,0:T(8,128)(2,1)} %pad_maximum_fusion.7), channel_id=1, source_target_pairs={{0,56},{8,0},{16,8},{24,16},{32,24},{40,32},{48,40},{56,48},{1,57}... | collective-permute-start | bytes 1572872 | tf_op jit(solution)/shard_map/ppermute | solution.py:39
  136.6 57.9 %collective-permute-start.33 = (bf16[16,128,256]{2,1,0:T(8,128)(2,1)}, bf16[16,128,256]{2,1,0:T(8,128)(2,1)}, u32[]{:S(2)}, u32[]{:S(2)}) collective-permute-start(bf16[16,128,256]{2,1,0:T(8,128)(2,1)} %pad_maximum_fusion.2), channel_id=1, source_target_pairs={{0,2},{2,4},{4,6},{6,0},{1,3},{3,5},{5,7},{7,1},{8,10},{10,12},{12... | collective-permute-start | bytes 3145736 | tf_op jit(solution)/shard_map/ppermute | solution.py:39
  153.9 86.0 %all-gather.5.cloned.1.call-start = ((), (), s32[]{:S(2)}) async-start(), calls=%async_computation.4 | async-start | bytes 1253376 | tf_op jit(solution)/shard_map/all_gather | solution.py:447
  155.8 38.6 %collective-permute-start.34 = (bf16[16,128,256]{2,1,0:T(8,128)(2,1)}, bf16[16,128,256]{2,1,0:T(8,128)(2,1)}, u32[]{:S(2)}, u32[]{:S(2)}) collective-permute-start(bf16[16,128,256]{2,1,0:T(8,128)(2,1)} %pad_maximum_fusion.3), channel_id=1, source_target_pairs={{0,6},{2,0},{4,2},{6,4},{1,7},{3,1},{5,3},{7,5},{8,14},{10,8},{12,... | collective-permute-start | bytes 3145736 | tf_op jit(solution)/shard_map/ppermute | solution.py:39
  158.2 36.2 %collective-permute-start.31 = (bf16[8,128,256]{2,1,0:T(8,128)(2,1)}, bf16[8,128,256]{2,1,0:T(8,128)(2,1)}, u32[]{:S(2)}, u32[]{:S(2)}) collective-permute-start(bf16[8,128,256]{2,1,0:T(8,128)(2,1)} %add_convert_fusion.7), channel_id=1, source_target_pairs={{0,8},{8,16},{16,24},{24,32},{32,40},{40,48},{48,56},{56,0},{1,9},... | collective-permute-start | bytes 1572872 | tf_op jit(solution)/shard_map/ppermute | solution.py:39
  160.3 34.1 %collective-permute-start.32 = (bf16[8,128,256]{2,1,0:T(8,128)(2,1)}, bf16[8,128,256]{2,1,0:T(8,128)(2,1)}, u32[]{:S(2)}, u32[]{:S(2)}) collective-permute-start(bf16[8,128,256]{2,1,0:T(8,128)(2,1)} %add_convert_fusion.6), channel_id=1, source_target_pairs={{0,56},{8,0},{16,8},{24,16},{32,24},{40,32},{48,40},{56,48},{1,57}... | collective-permute-start | bytes 1572872 | tf_op jit(solution)/shard_map/ppermute | solution.py:39
  191.6 91.1 %all-gather.7.cloned.1.call-start = ((), (), s32[]{:S(2)}) async-start(), calls=%async_computation.5 | async-start | bytes 1769472 | tf_op jit(solution)/shard_map/all_gather | solution.py:449
  193.0 22.2 %collective-permute-start.41 = (bf16[16,128,256]{2,1,0:T(8,128)(2,1)S(1)}, bf16[16,128,256]{2,1,0:T(8,128)(2,1)S(1)}, u32[]{:S(2)}, u32[]{:S(2)}) collective-permute-start(bf16[16,128,256]{2,1,0:T(8,128)(2,1)S(1)} %pad_maximum_fusion.4), channel_id=1, source_target_pairs={{0,64},{64,128},{128,192},{192,0},{1,65},{65,129},{129,193},{193,1... | collective-permute-start | bytes 3145736 | tf_op jit(solution)/shard_map/ppermute | solution.py:39
  196.4 53.6 %collective-permute-start.40 = (bf16[8,128,256]{2,1,0:T(8,128)(2,1)}, bf16[8,128,256]{2,1,0:T(8,128)(2,1)}, u32[]{:S(2)}, u32[]{:S(2)}) collective-permute-start(bf16[8,128,256]{2,1,0:T(8,128)(2,1)} %add_convert_fusion.2), channel_id=1, source_target_pairs={{0,56},{8,0},{16,8},{24,16},{32,24},{40,32},{48,40},{56,48},{1,57}... | collective-permute-start | bytes 1572872 | tf_op jit(solution)/shard_map/ppermute | solution.py:39
  199.6 9.4 %collective-permute-start.37 = (bf16[1,128,256]{2,1,0:T(8,128)(2,1)S(1)}, bf16[1,128,256]{2,1,0:T(8,128)(2,1)S(1)}, u32[]{:S(2)}, u32[]{:S(2)}) collective-permute-start(bf16[1,128,256]{2,1,0:T(8,128)(2,1)S(1)} %get-tuple-element.216), channel_id=1, source_target_pairs={{0,56},{8,0},{16,8},{24,16},{32,24},{40,32},{48,40},{56,48},{1,57}... | collective-permute-start | bytes 196616 | tf_op jit(solution)/shard_map/ppermute | solution.py:39
  202.3 47.7 %collective-permute-start.39 = (bf16[8,128,256]{2,1,0:T(8,128)(2,1)}, bf16[8,128,256]{2,1,0:T(8,128)(2,1)}, u32[]{:S(2)}, u32[]{:S(2)}) collective-permute-start(bf16[8,128,256]{2,1,0:T(8,128)(2,1)} %add_convert_fusion.3), channel_id=1, source_target_pairs={{0,8},{8,16},{16,24},{24,32},{32,40},{40,48},{48,56},{56,0},{1,9},... | collective-permute-start | bytes 1572872 | tf_op jit(solution)/shard_map/ppermute | solution.py:39
  203.7 38.0 %collective-permute-start.35 = (bf16[1,128,256]{2,1,0:T(8,128)(2,1)}, bf16[1,128,256]{2,1,0:T(8,128)(2,1)}, u32[]{:S(2)}, u32[]{:S(2)}) collective-permute-start(bf16[1,128,256]{2,1,0:T(8,128)(2,1)} %get-tuple-element.217), channel_id=1, source_target_pairs={{0,8},{8,16},{16,24},{24,32},{32,40},{40,48},{48,56},{56,0},{1,9},... | collective-permute-start | bytes 196616 | tf_op jit(solution)/shard_map/ppermute | solution.py:39
  209.0 9.4 %collective-permute-start.38 = (bf16[2,128,256]{2,1,0:T(8,128)(2,1)S(1)}, bf16[2,128,256]{2,1,0:T(8,128)(2,1)S(1)}, u32[]{:S(2)}, u32[]{:S(2)}) collective-permute-start(bf16[2,128,256]{2,1,0:T(8,128)(2,1)S(1)} %pad_maximum_fusion.12), channel_id=1, source_target_pairs={{0,56},{8,0},{16,8},{24,16},{32,24},{40,32},{48,40},{56,48},{1,57}... | collective-permute-start | bytes 393224 | tf_op jit(solution)/shard_map/ppermute | solution.py:39
  217.5 32.5 %collective-permute-start.42 = (bf16[16,128,256]{2,1,0:T(8,128)(2,1)S(1)}, bf16[16,128,256]{2,1,0:T(8,128)(2,1)}, u32[]{:S(2)}, u32[]{:S(2)}) collective-permute-start(bf16[16,128,256]{2,1,0:T(8,128)(2,1)S(1)} %pad_maximum_fusion.5), channel_id=1, source_target_pairs={{0,192},{64,0},{128,64},{192,128},{1,193},{65,1},{129,65},{193,129... | collective-permute-start | bytes 3145736 | tf_op jit(solution)/shard_map/ppermute | solution.py:39
  252.6 8.1 %collective-permute-start.44 = (bf16[2,128,256]{2,1,0:T(8,128)(2,1)S(1)}, bf16[2,128,256]{2,1,0:T(8,128)(2,1)S(1)}, u32[]{:S(2)}, u32[]{:S(2)}) collective-permute-start(bf16[2,128,256]{2,1,0:T(8,128)(2,1)S(1)} %get-tuple-element.182), channel_id=1, source_target_pairs={{0,56},{8,0},{16,8},{24,16},{32,24},{40,32},{48,40},{56,48},{1,57}... | collective-permute-start | bytes 393224 | tf_op jit(solution)/shard_map/ppermute | solution.py:39
  254.6 6.9 %collective-permute-start.43 = (bf16[2,128,256]{2,1,0:T(8,128)(2,1)S(1)}, bf16[2,128,256]{2,1,0:T(8,128)(2,1)S(1)}, u32[]{:S(2)}, u32[]{:S(2)}) collective-permute-start(bf16[2,128,256]{2,1,0:T(8,128)(2,1)S(1)} %add_convert_fusion.19), channel_id=1, source_target_pairs={{0,8},{8,16},{16,24},{24,32},{32,40},{40,48},{48,56},{56,0},{1,9},... | collective-permute-start | bytes 393224 | tf_op jit(solution)/shard_map/ppermute | solution.py:39
  262.7 6.6 %collective-permute-start.50 = (bf16[4,128,256]{2,1,0:T(8,128)(2,1)S(1)}, bf16[4,128,256]{2,1,0:T(8,128)(2,1)S(1)}, u32[]{:S(2)}, u32[]{:S(2)}) collective-permute-start(bf16[4,128,256]{2,1,0:T(8,128)(2,1)S(1)} %get-tuple-element.187), channel_id=1, source_target_pairs={{0,6},{2,0},{4,2},{6,4},{1,7},{3,1},{5,3},{7,5},{8,14},{10,8},{12,... | collective-permute-start | bytes 786440 | tf_op jit(solution)/shard_map/ppermute | solution.py:39
  265.4 7.6 %collective-permute-start.49 = (bf16[4,128,256]{2,1,0:T(8,128)(2,1)S(1)}, bf16[4,128,256]{2,1,0:T(8,128)(2,1)S(1)}, u32[]{:S(2)}, u32[]{:S(2)}) collective-permute-start(bf16[4,128,256]{2,1,0:T(8,128)(2,1)S(1)} %get-tuple-element.186), channel_id=1, source_target_pairs={{0,2},{2,4},{4,6},{6,0},{1,3},{3,5},{5,7},{7,1},{8,10},{10,12},{12... | collective-permute-start | bytes 786440 | tf_op jit(solution)/shard_map/ppermute | solution.py:39
  282.7 11.6 %collective-permute-start.52 = (f32[8,4,32,384]{3,2,1,0:T(8,128)}, f32[8,4,32,384]{3,2,1,0:T(8,128)}, u32[]{:S(2)}, u32[]{:S(2)}) collective-permute-start(f32[8,4,32,384]{3,2,1,0:T(8,128)} %bitcast.49), channel_id=1, source_target_pairs={{0,1},{1,0},{2,3},{3,2},{4,5},{5,4},{6,7},{7,6},{8,9},{9,8},{10,11... | collective-permute-start | bytes 4718600 | tf_op jit(solution)/shard_map/ppermute | solution.py:39
  282.7 9.4 %collective-permute-start.51 = (f32[2,128,256]{2,1,0:T(8,128)S(1)}, f32[2,128,256]{2,1,0:T(8,128)S(1)}, u32[]{:S(2)}, u32[]{:S(2)}) collective-permute-start(f32[2,128,256]{2,1,0:T(8,128)S(1)} %slice.378), channel_id=1, source_target_pairs={{0,1},{1,0},{2,3},{3,2},{4,5},{5,4},{6,7},{7,6},{8,9},{9,8},{10,11... | collective-permute-start | bytes 786440 | tf_op jit(solution)/shard_map/ppermute | solution.py:39
  285.8 6.3 %collective-permute-start.47 = (bf16[2,128,256]{2,1,0:T(8,128)(2,1)S(1)}, bf16[2,128,256]{2,1,0:T(8,128)(2,1)S(1)}, u32[]{:S(2)}, u32[]{:S(2)}) collective-permute-start(bf16[2,128,256]{2,1,0:T(8,128)(2,1)S(1)} %get-tuple-element.184), channel_id=1, source_target_pairs={{0,8},{8,16},{16,24},{24,32},{32,40},{40,48},{48,56},{56,0},{1,9},... | collective-permute-start | bytes 393224 | tf_op jit(solution)/shard_map/ppermute | solution.py:39
  (46 other events, 591.3 us)
Sparse Core Ops, SparseCore 0:
  48.3 31.6 reduce-scatter.2
  154.0 36.0 reduce-scatter.4
  192.8 47.0 all-gather.4
  242.2 40.3 all-gather.6
where the time goes:
time: 311 us; the launch traced here: 305 us
  waiting for transfers between devices  109 us (35%)
  starting transfers between devices  83.8 us (27%)
  Pallas kernels  35 us (11%)
  other arithmetic  34.4 us (11%)
  local copies, waits for them, and re-layouts  26.5 us (9%)
  between operations  15.4 us (5%)
    ppermute x53, starting transfers between devices, shift(): return lax.ppermute(value, axis, [(i, (i + k) % n) for i in range(n)])  83.6 us
    ppermute x53, waiting for transfers between devices, shift(): return lax.ppermute(value, axis, [(i, (i + k) % n) for i in range(n)])  53.9 us
    reduce_scatter x1, waiting for transfers between devices, body(): weights = lax.psum_scatter(weights, 'z', scatter_dimension=0, tiled=True)  25 us
    pallas_call x3, Pallas kernels, tile_sums(): pl.pallas_call(lambda *refs: tile_kernel(parts, *refs), out_shape=[jax.Sh...  23.2 us
    all_gather x1, waiting for transfers between devices, body(): lax.all_gather(weights, ('group', 'x'), axis=0)  20.3 us
    unnamed x75, local copies, waits for them, and re-layouts  16.4 us
    pallas_call x2, Pallas kernels, scalars(): pl.pallas_call(kernel, out_shape=[jax.ShapeDtypeStruct((n,), i32) for n i...  9.77 us
    all_gather x1, waiting for transfers between devices, body(): weights = lax.all_gather(weights, 'z', axis=0)  9.61 us
  transfers between devices with their start and end apart: 57, of which 23 were waited for; matrix products, arithmetic and copies ran while one was open for 13% of the time, Pallas kernels for 11%

commit v1 on v0

--- a/solution.py
+++ b/solution.py
@@ -16,7 +16,7 @@
 
 SEND, CROSS, HT, HS, FT, FS, FC, INTS = 0, 64, 72, 88, 104, 120, 136, 256
 HEAD = 16
-FIELDS, ENTRIES = 5, 160
+FIELDS, ENTRIES = 5, 161
 LIST = 1 + FIELDS * ENTRIES
 PICKED = 1 + 128
 
@@ -60,7 +60,7 @@
 
 
 def list_kernel(meta, row, picked, *refs):
-    heads, lists, (low, wide, words, sems) = refs[:11], refs[11:14], refs[14:]
+    heads, (out, low, wide, words, sems) = refs[:11], refs[11:]
     core, z, x, y = (meta[j] for j in range(4))
     copies = [pltpu.make_async_copy(v.at[pl.ds(0, HEAD)], low.at[j], sems.at[j]) for j, v in enumerate(heads)]
     for copy in copies:
@@ -71,8 +71,8 @@
     copy = pltpu.make_async_copy(wide.at[:, pl.ds(0, 8)], words, sems.at[0])
     copy.start()
     copy.wait()
-    for out in lists:
-        out[0] = 0
+    for group in range(3):
+        out[group * LIST] = 0
 
     def master(slot, dx, r):
         in_dom = slot < 66
@@ -109,27 +109,20 @@
         c = jnp.where(dy == 2, 24, jnp.where(dy == 1, 88, 104)) + r * 8 + dx * 2
         return live, jnp.where(dy > 0, c, jnp.where(same == 0, a, b)) + k
 
-    def append(tile_ref, tile, block_ref, start, place):
-        def into(out, place):
-            n = out[0]
-            out[0] = n + 1
-            for j, value in enumerate((tile_ref, tile, block_ref, start, place)):
-                out[1 + ENTRIES * j + n] = value
-
-        for out, begin, size in zip(lists, STARTS, SIZES):
-
-            @pl.when(jnp.logical_and(place >= begin, place < begin + size))
-            def _(out=out, begin=begin):
-                into(out, place - begin)
-
-    @pl.loop(0, 2 * NT)
+    def append(live, tile_ref, tile, block_ref, start, place):
+        middle, last = place >= STARTS[1], place >= STARTS[2]
+        base = jnp.where(last, 2 * LIST, jnp.where(middle, LIST, 0))
+        place = place - jnp.where(last, STARTS[2], jnp.where(middle, STARTS[1], 0))
+        n = out[base]
+        for j, value in enumerate((tile_ref, tile, block_ref, start, place)):
+            out[base + 1 + ENTRIES * j + n] = value
+        out[base] = n + live.astype(i32)
+
+    @pl.loop(0, 2 * NT, unroll=4)
     def _(i):
         r, t = i >> 4, i & 15
         live, place = accumulator(row[r * INTS + HS + t], 0, r)
-
-        @pl.when(live)
-        def _():
-            append(5 + r, t, 0, HEAD + BLK * (2 * r + row[r * INTS + HT + t]), place)
+        append(live, 5 + r, t, 0, HEAD + BLK * (2 * r + row[r * INTS + HT + t]), place)
 
     @pl.loop(0, picked[0])
     def _(i):
@@ -138,16 +131,14 @@
         base = (which >> 4) * INTS
         target_live, dy, dz, _, same, k = master(row[base + FT + t], dx, r)
         source_live, place = accumulator(row[base + FS + t], dx, r)
-
-        @pl.when(jnp.logical_and(target_live, source_live))
-        def _():
-            far = dz == 4
-            block_ref = jnp.where(far, 4 + same, jnp.where(dz > 4, dz + 1, dz))
-            block_ref = jnp.where(dy > 0, 12 - dy, block_ref)
-            j = jnp.where(far, k, 2 * same + k)
-            start = jnp.where(jnp.logical_and(far, same == 1), 0, HEAD) + BLK * j
-            tile_ref = jnp.where(dx == 2, 3 + r, jnp.where(dx == 3, 2, dx))
-            append(tile_ref, jnp.where(dx == 2, t, r * NT + t), block_ref, start, place)
+        far = dz == 4
+        block_ref = jnp.where(far, 4 + same, jnp.where(dz > 4, dz + 1, dz))
+        block_ref = jnp.where(dy > 0, 12 - dy, block_ref)
+        j = jnp.where(far, k, 2 * same + k)
+        start = jnp.where(jnp.logical_and(far, same == 1), 0, HEAD) + BLK * j
+        tile_ref = jnp.where(dx == 2, 3 + r, jnp.where(dx == 3, 2, dx))
+        live = jnp.logical_and(target_live, source_live)
+        append(live, tile_ref, jnp.where(dx == 2, t, r * NT + t), block_ref, start, place)
 
 
 bar = lax.optimization_barrier
@@ -157,40 +148,50 @@
     return lax.dot_general(tile, block, (((0,), (0,)), ((), ())), preferred_element_type=f32)
 
 
-def tile_kernel(parts, todo, *refs):
+def tile_kernel(group, todo, *refs):
+    parts, base = GROUPS[group], group * LIST
     tile_refs, block_refs, outs = refs[:7], refs[7:19], refs[19 : 19 + len(parts)]
     acc, tiles, blocks, tile_sems, block_sems, out_sems = refs[19 + len(parts) :]
-    n = todo[0]
+    n = todo[base]
 
     def held(c):
         return jnp.clip(n - c * SLOTS, 0, SLOTS)
 
+    def choose(which, options, low, act):
+        if len(options) == 1:
+            act(options[0])
+            return
+        cut = len(options) // 2
+
+        @pl.when(which < low + cut)
+        def _():
+            choose(which, options[:cut], low, act)
+
+        @pl.when(which >= low + cut)
+        def _():
+            choose(which, options[cut:], low + cut, act)
+
     def start(c):
         def one(j, _):
-            i = c * SLOTS + j
-            which, tile = todo[1 + i], todo[1 + ENTRIES + i]
-            for s, ref in enumerate(tile_refs):
-
-                @pl.when(which == s)
-                def _(ref=ref):
-                    pltpu.make_async_copy(ref.at[tile], tiles.at[j], tile_sems.at[j]).start()
-
-            which_block = todo[1 + 2 * ENTRIES + i]
-            at = pl.multiple_of(todo[1 + 3 * ENTRIES + i], 16)
-            for s, ref in enumerate(block_refs):
-
-                @pl.when(which_block == s)
-                def _(ref=ref):
-                    copy = pltpu.make_async_copy(ref.at[pl.ds(at, BLK)], blocks.at[j], block_sems.at[j])
-                    copy.start()
-
+            i = base + 1 + c * SLOTS + j
+            tile = todo[ENTRIES + i]
+            at = pl.multiple_of(todo[3 * ENTRIES + i], 16)
+
+            def fetch_tile(ref):
+                pltpu.make_async_copy(ref.at[tile], tiles.at[j], tile_sems.at[j]).start()
+
+            def fetch_block(ref):
+                pltpu.make_async_copy(ref.at[pl.ds(at, BLK)], blocks.at[j], block_sems.at[j]).start()
+
+            choose(todo[i], tile_refs, 0, fetch_tile)
+            choose(todo[2 * ENTRIES + i], block_refs, 0, fetch_block)
             return 0
 
         lax.fori_loop(0, held(c), one, 0)
 
     def finish(c):
         def one(j, _):
-            place = todo[1 + 4 * ENTRIES + c * SLOTS + j]
+            place = todo[base + 1 + 4 * ENTRIES + c * SLOTS + j]
             pltpu.make_async_copy(tile_refs[0].at[0], tiles.at[j], tile_sems.at[j]).wait()
             pltpu.make_async_copy(block_refs[0].at[pl.ds(0, BLK)], blocks.at[j], block_sems.at[j]).wait()
             term = tile_product(tiles[j], blocks[j])
@@ -224,10 +225,10 @@
 def tile_sums(group, todo, tile_refs, block_refs):
     parts, size = GROUPS[group], SIZES[group]
     return pl.pallas_call(
-        lambda *refs: tile_kernel(parts, *refs),
+        lambda *refs: tile_kernel(group, *refs),
         out_shape=[jax.ShapeDtypeStruct((m, BLK, HALF), bf16) for _, m in parts],
         in_specs=[SMEM] + [ANY] * 19,
-        out_specs=[HBM] * len(parts),
+        out_specs=[ANY] * len(parts),
         scratch_shapes=[
             pltpu.VMEM((size, BLK, HALF), bf16),
             pltpu.VMEM((SLOTS, BLK, BLK), bf16),
@@ -239,6 +240,63 @@
         compiler_params=pltpu.CompilerParams(vmem_limit_bytes=10 * MIB),
         cost_estimate=pl.CostEstimate(flops=10**9, bytes_accessed=2 * 10**7, transcendentals=0),
     )(todo, *tile_refs, *block_refs)
+
+
+def join_kernel(head, own, sib, out):
+    out[:HEAD] = head[...]
+    out[HEAD : HEAD + HALF] = own[...]
+    out[HEAD + HALF :] = sib[...]
+
+
+def join_chunk(head, own, sib):
+    return pl.pallas_call(
+        join_kernel,
+        out_shape=jax.ShapeDtypeStruct((HEAD + 2 * HALF, HALF), bf16),
+        in_specs=[VMEM] * 3,
+        out_specs=VMEM,
+        compiler_params=pltpu.CompilerParams(vmem_limit_bytes=4 * MIB),
+    )(head, own, sib)
+
+
+def weight_kernel(meta, grad_pre, feats, neigh, mine, other, source, sums, sems):
+    loads = [pltpu.make_async_copy(v, source.at[j], sems.at[j]) for j, v in enumerate((feats, neigh))]
+    for load in loads:
+        load.start()
+    core = meta[0]
+    low, high = grad_pre[:, :HALF], grad_pre[:, HALF:]
+    for load in loads:
+        load.wait()
+    stores = []
+    for j, (out, from_low) in enumerate(((other, core == 1), (mine, core == 0))):
+        part = jnp.where(from_low, low, high)
+        bias = jnp.sum(part.astype(f32), axis=0, keepdims=True)
+        for g in range(NY):
+            cols = source[g // 2, :, (g % 2) * HALF : (g % 2 + 1) * HALF]
+            sums[j, g, :, :HALF] = tile_product(cols, part)
+            sums[j, g, :, HALF:] = jnp.zeros((HALF, BLK), f32)
+            if g == 0:
+                sums[j, g, 0:1, HALF:] = bias[:, :BLK]
+                sums[j, g, 1:2, HALF:] = bias[:, BLK:]
+        stores.append(pltpu.make_async_copy(sums.at[j], out, sems.at[2 + j]))
+        stores[-1].start()
+    for store in stores:
+        store.wait()
+
+
+def weight_terms(meta, feats, neigh, grad_pre):
+    shape = (NY, HALF, HALF + BLK)
+    return pl.pallas_call(
+        weight_kernel,
+        out_shape=[jax.ShapeDtypeStruct(shape, f32)] * 2,
+        in_specs=[SMEM, VMEM, HBM, HBM],
+        out_specs=[HBM] * 2,
+        scratch_shapes=[
+            pltpu.VMEM((2, *feats.shape), bf16),
+            pltpu.VMEM((2, *shape), f32),
+            pltpu.SemaphoreType.DMA((4,)),
+        ],
+        compiler_params=pltpu.CompilerParams(vmem_limit_bytes=8 * MIB),
+    )(meta, grad_pre, feats, neigh)
 
 
 def agg_kernel(meta, pre_act, cotan, w_neigh, grad_pre, agg_own, agg_other):
@@ -331,24 +389,25 @@
     return jnp.concatenate([value[:n].astype(bf16), add(value[n:], tail).astype(bf16)])
 
 
-def return_sums(first, sums_of):
+def return_sums(first, sums_of, weights):
     a2h, a2t, b4h, b4t, y2h, y2t = first
-    b4h, b4t, a2h, a2t, (a1, a3, b3, b5, y1, y3) = sums_of(1, (b4h, b4t, a2h, a2t))
+    w = next(weights)
+    b4h, b4t, a2h, a2t, y2h, y2t, w, (a1, a3, b3, b5, y1, y3) = sums_of(1, (b4h, b4t, a2h, a2t, y2h, y2t, w))
+    w = weights.send(w)
     up, down = shift(b4h, "z", 1), shift(b4t, "z", -1)
     ax_p, ax_m = shift(a2h, "x", 1), shift(a2t, "x", -1)
-    up, down, y2h, y2t = bar((up, down, y2h, y2t))
-    y_p, y_m = shift(y2h, "group", 1), shift(y2t, "group", -1)
-
-    up, down, ax_p, ax_m, a1, a3, b3, b5 = bar((up, down, ax_p, ax_m, a1, a3, b3, b5))
-    up, down, ax_p, ax_m, (a0, b0, b1, b2, b6, b7) = sums_of(2, (up, down, ax_p, ax_m))
+    y_p = shift(y2h, "group", 1)
+
+    up, down, ax_p, ax_m, y_p, y2t, a1, a3, b3, b5 = bar((up, down, ax_p, ax_m, y_p, y2t, a1, a3, b3, b5))
+    up, down, ax_p, ax_m, y2t, (a0, b0, b1, b2, b6, b7) = sums_of(2, (up, down, ax_p, ax_m, y2t))
+    up, down = shift(add_head(b3, up), "z", 1), shift(add_tail(b5, down), "z", -1)
     ax_p, ax_m = shift(add_head(a1, ax_p), "x", 1), shift(add_tail(a3, ax_m), "x", -1)
-    up, down = shift(add_head(b3, up), "z", 1), shift(add_tail(b5, down), "z", -1)
-    up, down, y_p, y_m = bar((up, down, y_p, y_m))
+    y_m = shift(y2t, "group", -1)
+
+    up, down, y_p, y_m, b2, b6 = bar((up, down, y_p, y_m, b2, b6))
     up, down = add(b2, up).astype(bf16), add(b6, down).astype(bf16)
     up, down = shift(up, "z", 1), shift(down, "z", -1)
     y_p = shift(add_head(y1, y_p), "group", 1)
-    y_p, y_m = bar((y_p, y_m))
-    y_m = shift(add_tail(y3, y_m), "group", -1)
 
     def part_a(dz):
         rows = slice(2 * dz, 2 * dz + 2)
@@ -360,11 +419,13 @@
         sums = add(b0[rows], up[rows], down[rows], y_p[cross], y_m[cross])
         return jnp.concatenate([sums, add(y_p[rows], y_m[rows])])
 
-    up, down, ax_p, ax_m = bar((up, down, ax_p, ax_m))
+    up, down, ax_p, ax_m, y_p, y_m, w = bar((up, down, ax_p, ax_m, y_p, y_m, w))
+    w = weights.send(w)
     far = part_a(4).astype(bf16)
     up, down = add(b1, up).astype(bf16), add(b7, down).astype(bf16)
     az_p, az_m = shift(far[:1], "z", 1), shift(far[1:], "z", -1)
     up, down = shift(up, "z", 1), shift(down, "z", -1)
+    y_m = shift(add_tail(y3, y_m), "group", -1)
     az_p, az_m = add_head(part_a(3), az_p), add_tail(part_a(5), az_m)
     az_p, az_m = shift(az_p, "z", 1), shift(az_m, "z", -1)
     az_p, az_m = add(part_a(2), az_p).astype(bf16), add(part_a(6), az_m).astype(bf16)
@@ -378,7 +439,7 @@
     bx_p, bx_m = shift(bx_p, "x", 1), shift(bx_m, "x", -1)
     az_p, az_m = shift(az_p, "z", 1), shift(az_m, "z", -1)
     sum_b = add(part_b(0), bx_p, bx_m)
-    return add(part_a(0), az_p, az_m, sum_b[2:]), sum_b[:2]
+    return add(part_a(0), az_p, az_m, sum_b[2:]), sum_b[:2], w
 
 
 def body(
@@ -426,9 +487,14 @@
         low, high = jnp.where(first_core, mine, other), jnp.where(first_core, other, mine)
         return jnp.concatenate([low, high], axis=-1)
 
-    grad_pre, agg_own, agg_other = agg_terms(meta, pre_act, cotan, w_neigh)
+    grad_pre = jnp.where(pre_act > 0, cotan, jnp.zeros_like(cotan))
+    wn_mine = lax.dynamic_slice_in_dim(w_neigh, core * HALF, HALF)
+    wn_other = lax.dynamic_slice_in_dim(w_neigh, (1 - core) * HALF, HALF)
+    agg_other = lax.dot_general(grad_pre, wn_other, cols, preferred_element_type=f32).astype(bf16)
+    agg_sib = shift(agg_other, "core", 1)
+    agg_own = lax.dot_general(grad_pre, wn_mine, cols, preferred_element_type=f32).astype(bf16)
     head = jnp.concatenate([words, cross_words, jnp.zeros((HEAD - 3, HALF), bf16)])
-    chunk = join_chunk(head, agg_own, shift(agg_other, "core", 1))
+    chunk = join_chunk(head, agg_own, agg_sib)
 
     far_own, home_own = far_tiles[0, 0], home_tiles[0, 0]
     mine, other = weight_terms(meta, feats, neigh, grad_pre)
@@ -442,30 +508,35 @@
     up1, dn1, chunk, row, mine, other = bar((up1, dn1, chunk, row, mine, other))
     weights = (mine + other).reshape(4 * HALF, HALF + BLK)
     weights = lax.psum_scatter(weights, "group", scatter_dimension=0, tiled=True)
-    weights = lax.psum_scatter(weights, "z", scatter_dimension=0, tiled=True)
-    weights = jnp.pad(weights, ((0, 16), (0, 0)))
-    weights = lax.all_gather(weights, ("group", "x"), axis=0).reshape(NY, NX, 48, HALF + BLK)
-    weights = jnp.sum(weights[:, :, :32], axis=1)
-    weights = lax.all_gather(weights, "z", axis=0)
     up2, dn2 = shift(up1, "z", 1), shift(dn1, "z", -1)
     y1 = shift(chunk, "group", 1)
     (picked,) = scalars(pick_kernel, (PICKED,), meta, row)
-    up2, dn2, y1, tiles1, tiles3, chunk, picked = bar((up2, dn2, y1, tiles1, tiles3, chunk, picked))
+    up2, dn2, tiles1, tiles3, picked = bar((up2, dn2, tiles1, tiles3, picked))
     up3, dn3 = shift(up2, "z", 1), shift(dn2, "z", -1)
     tiles2h, tiles2t = shift(tiles3[:NT], "x", 1), shift(tiles1[NT:], "x", -1)
+    y1, chunk = bar((y1, chunk))
     y3 = shift(chunk, "group", 3)
-    up3, dn3, y3, chunk = bar((up3, dn3, y3, chunk))
+    up3, dn3, weights = bar((up3, dn3, weights))
+    weights = lax.psum_scatter(weights, "z", scatter_dimension=0, tiled=True)
     middle = HEAD + 2 * BLK
     up4, dn4 = shift(up3[:middle], "z", 1), shift(dn3[middle:], "z", -1)
+    y3, chunk = bar((y3, chunk))
     y2 = shift(chunk, "group", 2)
     up4, dn4, tiles2h, tiles2t, y2 = bar((up4, dn4, tiles2h, tiles2t, y2))
+
+    def weight_stages(w):
+        w = yield w
+        w = jnp.pad(w, ((0, 16), (0, 0)))
+        w = yield lax.all_gather(w, ("group", "x"), axis=0)
+        w = jnp.sum(w.reshape(NY, NX, 48, HALF + BLK)[:, :, :32], axis=1)
+        yield lax.all_gather(w, "z", axis=0)
 
     tile_refs = [far_both, tiles1, tiles3, tiles2h, tiles2t, home_own, home_sib]
     block_refs = [chunk, dn1, dn2, dn3, up4, dn4, up3, up2, up1, y1, y2, y3]
     heads = [chunk, dn1, dn2, dn3, up4, up3, up2, up1, y1, y2, y3]
-    todo = scalars(
+    (todo,) = scalars(
         list_kernel,
-        (LIST,) * 3,
+        (3 * LIST,),
         meta,
         row,
         picked,
@@ -479,11 +550,11 @@
     )
 
     def sums_of(group, arrived):
-        *arrived, now = bar((*arrived, todo[group]))
+        *arrived, now = bar((*arrived, todo))
         return *arrived, tile_sums(group, now, tile_refs, block_refs)
 
     (first,) = sums_of(0, ())
-    sum_a, sum_b = return_sums(first, sums_of)
+    sum_a, sum_b, weights = return_sums(first, sums_of, weight_stages(weights))
     self_grad = lax.dot_general(grad_pre, w_self, cols, preferred_element_type=f32)
     weights, sum_b = bar((weights, sum_b))
     other = shift(sum_b, "core", 1)

time: 311 us -> 304 us (0.977)
  the two profiles are of different devices: /device:TPU:16 before, /device:TPU:1 now
where the time goes in v1:
time: 304 us; the launch traced here: 298 us
  waiting for transfers between devices  94.5 us (31%)
  starting transfers between devices  91 us (30%)
  local copies, waits for them, and re-layouts  34.2 us (11%)
  Pallas kernels  30.9 us (10%)
  other arithmetic  29.6 us (10%)
  between operations  16.1 us (5%)
    ppermute x53, waiting for transfers between devices, shift(): return lax.ppermute(value, axis, [(i, (i + k) % n) for i in range(n)])  94.4 us
    ppermute x53, starting transfers between devices, shift(): return lax.ppermute(value, axis, [(i, (i + k) % n) for i in range(n)])  90.8 us
    unnamed x179, local copies, waits for them, and re-layouts  26 us
    pallas_call x3, Pallas kernels, tile_sums(): pl.pallas_call(lambda *refs: tile_kernel(group, *refs), out_shape=[jax.Sh...  20.8 us
    pallas_call x2, Pallas kernels, scalars(): pl.pallas_call(kernel, out_shape=[jax.ShapeDtypeStruct((n,), i32) for n i...  9.05 us
  transfers between devices with their start and end apart: 57, of which 22 were waited for; matrix products, arithmetic and copies ran while one was open for 11% of the time, Pallas kernels for 10%

profile of v1, /device:TPU:1, one launch (start us, length us, event | category | flops | bytes accessed | tf_op | source)
XLA Modules:
  0.0 297.9 jit_solution(15259588670993459754)
XLA Ops:
  10.4 2.1 collective-permute-start.2
  12.4 2.5 collective-permute-start.1
  17.4 1.6 collective-permute-start.4
  25.8 1.7 collective-permute-start.7
  27.5 3.9 %collective-permute-start.8 = (bf16[528,256]{1,0:T(8,128)(2,1)S(1)}, bf16[528,256]{1,0:T(8,128)(2,1)S(1)}, u32[]{:S(2)}, u32[]{:S(2)}) collective-permute-start(bf16[528,256]{1,0:T(8,128)(2,1)S(1)} %shard_map.192.refs_0_.refs_8_), channel_id=1, source_target_pairs={{0,56},{8,0},{16,8},{24,16},{32,24},{40,32},{48,40},{56,48},{1,57}... | collective-permute-start | bytes 811016 | tf_op jit(solution)/shard_map/ppermute | solution.py:39
  31.4 6.7 %collective-permute-done.7.refs_7_.refs_16_ = bf16[528,256]{1,0:T(8,128)(2,1)S(1)} collective-permute-done((bf16[528,256]{1,0:T(8,128)(2,1)S(1)}, bf16[528,256]{1,0:T(8,128)(2,1)S(1)}, u32[]{:S(2)}, u32[]{:S(2)}) %collective-permute-start.7) | collective-permute-done | bytes 270368 | tf_op jit(solution)/shard_map/ppermute | solution.py:39
  39.6 1.6 collective-permute-start.12
  41.2 2.7 collective-permute-start.11
  43.9 2.1 shard_map.194.picked
  46.6 17.2 %collective-permute-done.12.refs_2_ = bf16[32,128,128]{2,1,0:T(8,128)(2,1)S(1)} collective-permute-done((bf16[32,128,128]{2,1,0:T(8,128)(2,1)S(1)}, bf16[32,128,128]{2,1,0:T(8,128)(2,1)S(1)}, u32[]{:S(2)}, u32[]{:S(2)}) %collective-permute-start.12) | collective-permute-done | bytes 1048608 | tf_op jit(solution)/shard_map/ppermute | solution.py:39
  63.8 2.0 collective-permute-done.13.refs_3_
  66.6 3.0 collective-permute-start.17
  73.2 3.7 %collective-permute-done.14.refs_8_.refs_17_ = bf16[528,256]{1,0:T(8,128)(2,1)} collective-permute-done((bf16[528,256]{1,0:T(8,128)(2,1)S(1)}, bf16[528,256]{1,0:T(8,128)(2,1)}, u32[]{:S(2)}, u32[]{:S(2)}) %collective-permute-start.14) | collective-permute-done | bytes 270368 | tf_op jit(solution)/shard_map/ppermute | solution.py:39
  78.6 2.7 collective-permute-start.21
  82.2 1.7 collective-permute-start.22
  85.9 2.7 collective-permute-start.19
  89.1 1.6 collective-permute-done.19.refs_13_
  90.9 6.9 %shard_map.195.refs_0_ = s32[2418]{0:T(1024)S(1)} custom-call(s32[4]{0:T(128)S(1)} %copy-done.72, s32[2048]{0:T(1024)S(1)} %bitcast.46, s32[129]{0:T(256)S(1)} %copy-done.74, bf16[528,256]{1,0:T(8,128)(2,1)S(1)} %shard_map.192.refs_0_.refs_8_, bf16[528,256]{1,0:T(8,128)(2,1)S(1)} %copy-done.23, bf16[528,256]{1,0:T(8,128)(2,1)S(1)} %copy-done.31, ...), custom_call_target="tpu_custom_call" | custom-call | tf_op jit(solution)/shard_map/pallas_call | solution.py:365
  97.9 4.7 %shard_map.196 = (bf16[8,128,256]{2,1,0:T(8,128)(2,1)S(1)}, bf16[8,128,256]{2,1,0:T(8,128)(2,1)S(1)}, bf16[4,128,256]{2,1,0:T(8,128)(2,1)S(1)}, bf16[4,128,256]{...) custom-call(s32[2418]{0:T(1024)S(1)} %shard_map.195.refs_0_, ...), custom_call_target="tpu_custom_call" | custom-call | flops 1000000000 | bytes 20000000 | tf_op jit(solution)/shard_map/pallas_call | solution.py:227
  107.8 2.9 collective-permute-start.26
  111.4 3.6 %collective-permute-start.24 = (bf16[4,128,256]{2,1,0:T(8,128)(2,1)}, bf16[4,128,256]{2,1,0:T(8,128)(2,1)}, u32[]{:S(2)}, u32[]{:S(2)}) collective-permute-start(bf16[4,128,256]{2,1,0:T(8,128)(2,1)} %copy-done.81), channel_id=1, source_target_pairs={{0,56},{8,0},{16,8},{24,16},{32,24},{40,32},{48,40},{56,48},{1,57}... | collective-permute-start | bytes 786440 | tf_op jit(solution)/shard_map/ppermute | solution.py:39
  126.4 8.4 %shard_map.197 = (bf16[16,128,256]{2,1,0:T(8,128)(2,1)S(1)}, bf16[16,128,256]{2,1,0:T(8,128)(2,1)S(1)}, bf16[8,128,256]{2,1,0:T(8,128)(2,1)S(1)}, bf16[8,128,256...) custom-call(s32[2418]{0:T(1024)S(1)} %copy-done.67, ...), custom_call_target="tpu_custom_call" | custom-call | flops 1000000000 | bytes 20000000 | tf_op jit(solution)/shard_map/pallas_call | solution.py:227
  142.4 9.0 %collective-permute-start.28 = (bf16[8,128,256]{2,1,0:T(8,128)(2,1)S(1)}, bf16[8,128,256]{2,1,0:T(8,128)(2,1)S(1)}, u32[]{:S(2)}, u32[]{:S(2)}) collective-permute-start(bf16[8,128,256]{2,1,0:T(8,128)(2,1)S(1)} %pad_maximum_fusion.6), channel_id=1, source_target_pairs={{0,8},{8,16},{16,24},{24,32},{32,40},{40,48},{48,56},{56,0},{1,9},... | collective-permute-start | bytes 1572872 | tf_op jit(solution)/shard_map/ppermute | solution.py:39
  152.5 2.7 collective-permute-start.29
  155.2 5.3 %collective-permute-start.30 = (bf16[8,128,256]{2,1,0:T(8,128)(2,1)S(1)}, bf16[8,128,256]{2,1,0:T(8,128)(2,1)S(1)}, u32[]{:S(2)}, u32[]{:S(2)}) collective-permute-start(bf16[8,128,256]{2,1,0:T(8,128)(2,1)S(1)} %copy-done.77), channel_id=1, source_target_pairs={{0,192},{64,0},{128,64},{192,128},{1,193},{65,1},{129,65},{193,129... | collective-permute-start | bytes 1572872 | tf_op jit(solution)/shard_map/ppermute | solution.py:39
  163.6 2.7 collective-permute-start.34
  166.4 7.7 %shard_map.198 = (bf16[16,128,256]{2,1,0:T(8,128)(2,1)S(1)}, bf16[8,128,256]{2,1,0:T(8,128)(2,1)S(1)}, bf16[8,128,256]{2,1,0:T(8,128)(2,1)S(1)}, bf16[8,128,256]...) custom-call(s32[2418]{0:T(1024)S(1)} %copy-done.68, ...), custom_call_target="tpu_custom_call" | custom-call | flops 1000000000 | bytes 20000000 | tf_op jit(solution)/shard_map/pallas_call | solution.py:227
  174.3 1.8 add_convert_fusion.3
  178.2 1.6 collective-permute-start.32
  179.8 1.9 collective-permute-done.33
  181.9 4.6 %collective-permute-done.31 = bf16[8,128,256]{2,1,0:T(8,128)(2,1)} collective-permute-done((bf16[8,128,256]{2,1,0:T(8,128)(2,1)S(1)}, bf16[8,128,256]{2,1,0:T(8,128)(2,1)}, u32[]{:S(2)}, u32[]{:S(2)}) %collective-permute-start.31) | collective-permute-done | bytes 524320 | tf_op jit(solution)/shard_map/ppermute | solution.py:39
  186.7 13.0 %collective-permute-done.35 = bf16[16,128,256]{2,1,0:T(8,128)(2,1)} collective-permute-done((bf16[16,128,256]{2,1,0:T(8,128)(2,1)S(1)}, bf16[16,128,256]{2,1,0:T(8,128)(2,1)}, u32[]{:S(2)}, u32[]{:S(2)}) %collective-permute-start.35) | collective-permute-done | bytes 1048608 | tf_op jit(solution)/shard_map/ppermute | solution.py:39
  199.7 1.9 slice_reduce_fusion
  204.1 4.5 %collective-permute-start.38 = (bf16[1,128,256]{2,1,0:T(8,128)(2,1)S(1)}, bf16[1,128,256]{2,1,0:T(8,128)(2,1)S(1)}, u32[]{:S(2)}, u32[]{:S(2)}) collective-permute-start(bf16[1,128,256]{2,1,0:T(8,128)(2,1)S(1)} %get-tuple-element.216), channel_id=1, source_target_pairs={{0,56},{8,0},{16,8},{24,16},{32,24},{40,32},{48,40},{56,48},{1,57}... | collective-permute-start | bytes 196616 | tf_op jit(solution)/shard_map/ppermute | solution.py:39
  210.1 3.1 %collective-permute-start.39 = (bf16[2,128,256]{2,1,0:T(8,128)(2,1)S(1)}, bf16[2,128,256]{2,1,0:T(8,128)(2,1)S(1)}, u32[]{:S(2)}, u32[]{:S(2)}) collective-permute-start(bf16[2,128,256]{2,1,0:T(8,128)(2,1)S(1)} %pad_maximum_fusion.12), channel_id=1, source_target_pairs={{0,56},{8,0},{16,8},{24,16},{32,24},{40,32},{48,40},{56,48},{1,57}... | collective-permute-start | bytes 393224 | tf_op jit(solution)/shard_map/ppermute | solution.py:39
  214.7 12.8 %collective-permute-done.39 = bf16[2,128,256]{2,1,0:T(8,128)(2,1)S(1)} collective-permute-done((bf16[2,128,256]{2,1,0:T(8,128)(2,1)S(1)}, bf16[2,128,256]{2,1,0:T(8,128)(2,1)S(1)}, u32[]{:S(2)}, u32[]{:S(2)}) %collective-permute-start.39) | collective-permute-done | bytes 131104 | tf_op jit(solution)/shard_map/ppermute | solution.py:39
  228.7 6.9 %collective-permute-done.36 = bf16[1,128,256]{2,1,0:T(8,128)(2,1)S(1)} collective-permute-done((bf16[1,128,256]{2,1,0:T(8,128)(2,1)S(1)}, bf16[1,128,256]{2,1,0:T(8,128)(2,1)S(1)}, u32[]{:S(2)}, u32[]{:S(2)}) %collective-permute-start.36) | collective-permute-done | bytes 65568 | tf_op jit(solution)/shard_map/ppermute | solution.py:39
  235.7 9.1 %collective-permute-done.37 = bf16[2,128,256]{2,1,0:T(8,128)(2,1)S(1)} collective-permute-done((bf16[2,128,256]{2,1,0:T(8,128)(2,1)S(1)}, bf16[2,128,256]{2,1,0:T(8,128)(2,1)S(1)}, u32[]{:S(2)}, u32[]{:S(2)}) %collective-permute-start.37) | collective-permute-done | bytes 131104 | tf_op jit(solution)/shard_map/ppermute | solution.py:39
  248.7 2.6 collective-permute-start.46
  255.0 1.9 add_convert_fusion.14
  256.9 2.4 collective-permute-start.50
  259.3 3.4 %collective-permute-done.50 = bf16[4,128,256]{2,1,0:T(8,128)(2,1)S(1)} collective-permute-done((bf16[4,128,256]{2,1,0:T(8,128)(2,1)S(1)}, bf16[4,128,256]{2,1,0:T(8,128)(2,1)S(1)}, u32[]{:S(2)}, u32[]{:S(2)}) %collective-permute-start.50) | collective-permute-done | bytes 262176 | tf_op jit(solution)/shard_map/ppermute | solution.py:39
  262.7 3.0 %collective-permute-done.49 = bf16[4,128,256]{2,1,0:T(8,128)(2,1)S(1)} collective-permute-done((bf16[4,128,256]{2,1,0:T(8,128)(2,1)S(1)}, bf16[4,128,256]{2,1,0:T(8,128)(2,1)S(1)}, u32[]{:S(2)}, u32[]{:S(2)}) %collective-permute-start.49) | collective-permute-done | bytes 262176 | tf_op jit(solution)/shard_map/ppermute | solution.py:39
  266.5 13.0 %collective-permute-start.52 = (f32[8,4,32,384]{3,2,1,0:T(8,128)}, f32[8,4,32,384]{3,2,1,0:T(8,128)S(1)}, u32[]{:S(2)}, u32[]{:S(2)}) collective-permute-start(f32[8,4,32,384]{3,2,1,0:T(8,128)} %bitcast.52), channel_id=1, source_target_pairs={{0,1},{1,0},{2,3},{3,2},{4,5},{5,4},{6,7},{7,6},{8,9},{9,8},{10,11... | collective-permute-start | bytes 4718600 | tf_op jit(solution)/shard_map/ppermute | solution.py:39
  281.1 1.5 copy.31
  282.6 1.8 collective-permute-done.48
  284.5 1.8 collective-permute-done.47
  288.9 1.6 pad_maximum_fusion
  (335 shorter events, 74.0 us)
Async XLA Ops:
  7.2 65.8 %reduce-scatter.3.cloned.1.call-start = ((), (), s32[]{:S(2)}) async-start(), calls=%async_computation.2 | async-start | bytes 1966080 | tf_op jit(solution)/shard_map/reduce_scatter | solution.py:510
  10.4 9.0 %collective-permute-start.2 = (s32[256]{0:T(256)S(1)}, s32[256]{0:T(256)S(1)}, u32[]{:S(2)}, u32[]{:S(2)}) collective-permute-start(s32[256]{0:T(256)S(1)} %concatenate.55), channel_id=1, source_target_pairs={{0,2},{2,4},{4,6},{6,0},{1,3},{3,5},{5,7},{7,1},{8,10},{10,12},{12... | collective-permute-start | bytes 3080 | tf_op jit(solution)/shard_map/ppermute | solution.py:39
  12.4 7.5 %collective-permute-start.1 = (s32[256]{0:T(256)S(1)}, s32[256]{0:T(256)S(1)}, u32[]{:S(2)}, u32[]{:S(2)}) collective-permute-start(s32[256]{0:T(256)S(1)} %concatenate.55), channel_id=1, source_target_pairs={{0,4},{2,6},{4,0},{6,2},{1,5},{3,7},{5,1},{7,3},{8,12},{10,14},{12... | collective-permute-start | bytes 3080 | tf_op jit(solution)/shard_map/ppermute | solution.py:39
  17.4 6.6 %collective-permute-start.4 = (bf16[256,256]{1,0:T(8,128)(2,1)S(1)}, bf16[256,256]{1,0:T(8,128)(2,1)S(1)}, u32[]{:S(2)}, u32[]{:S(2)}) collective-permute-start(bf16[256,256]{1,0:T(8,128)(2,1)S(1)} %convolution_convert_fusion), channel_id=1, source_target_pairs={{0,1},{1,0},{2,3},{3,2},{4,5},{5,4},{6,7},{7,6},{8,9},{9,8},{10,11... | collective-permute-start | bytes 393224 | tf_op jit(solution)/shard_map/ppermute | solution.py:39
  19.4 5.9 %collective-permute-start.6 = (bf16[16,128,128]{2,1,0:T(8,128)(2,1)S(1)}, bf16[16,128,128]{2,1,0:T(8,128)(2,1)S(1)}, u32[]{:S(2)}, u32[]{:S(2)}) collective-permute-start(bf16[16,128,128]{2,1,0:T(8,128)(2,1)S(1)} %bitcast.41), channel_id=1, source_target_pairs={{0,1},{1,0},{2,3},{3,2},{4,5},{5,4},{6,7},{7,6},{8,9},{9,8},{10,11... | collective-permute-start | bytes 1572872 | tf_op jit(solution)/shard_map/ppermute | solution.py:39
  25.3 12.8 %collective-permute-start.9 = (f32[4,256,384]{2,1,0:T(8,128)}, f32[4,256,384]{2,1,0:T(8,128)S(1)}, u32[]{:S(2)}, u32[]{:S(2)}) collective-permute-start(f32[4,256,384]{2,1,0:T(8,128)} %copy-done.75), channel_id=1, source_target_pairs={{0,1},{1,0},{2,3},{3,2},{4,5},{5,4},{6,7},{7,6},{8,9},{9,8},{10,11... | collective-permute-start | bytes 4718600 | tf_op jit(solution)/shard_map/ppermute | solution.py:39
  25.8 12.3 %collective-permute-start.7 = (bf16[528,256]{1,0:T(8,128)(2,1)S(1)}, bf16[528,256]{1,0:T(8,128)(2,1)S(1)}, u32[]{:S(2)}, u32[]{:S(2)}) collective-permute-start(bf16[528,256]{1,0:T(8,128)(2,1)S(1)} %shard_map.192.refs_0_.refs_8_), channel_id=1, source_target_pairs={{0,8},{8,16},{16,24},{24,32},{32,40},{40,48},{48,56},{56,0},{1,9},... | collective-permute-start | bytes 811016 | tf_op jit(solution)/shard_map/ppermute | solution.py:39
  27.5 10.7 %collective-permute-start.8 = (bf16[528,256]{1,0:T(8,128)(2,1)S(1)}, bf16[528,256]{1,0:T(8,128)(2,1)S(1)}, u32[]{:S(2)}, u32[]{:S(2)}) collective-permute-start(bf16[528,256]{1,0:T(8,128)(2,1)S(1)} %shard_map.192.refs_0_.refs_8_), channel_id=1, source_target_pairs={{0,56},{8,0},{16,8},{24,16},{32,24},{40,32},{48,40},{56,48},{1,57}... | collective-permute-start | bytes 811016 | tf_op jit(solution)/shard_map/ppermute | solution.py:39
  39.6 68.3 %reduce-scatter.5.cloned.1.call-start = ((), (), s32[]{:S(2)}) async-start(), calls=%async_computation.3 | async-start | bytes 442368 | tf_op jit(solution)/shard_map/reduce_scatter | solution.py:520
  39.6 24.2 %collective-permute-start.12 = (bf16[32,128,128]{2,1,0:T(8,128)(2,1)S(1)}, bf16[32,128,128]{2,1,0:T(8,128)(2,1)S(1)}, u32[]{:S(2)}, u32[]{:S(2)}) collective-permute-start(bf16[32,128,128]{2,1,0:T(8,128)(2,1)S(1)} %pad_maximum_fusion.1.refs_1_), channel_id=1, source_target_pairs={{0,6},{2,0},{4,2},{6,4},{1,7},{3,1},{5,3},{7,5},{8,14},{10,8},{12,... | collective-permute-start | bytes 3145736 | tf_op jit(solution)/shard_map/ppermute | solution.py:39
  41.2 24.7 %collective-permute-start.13 = (bf16[32,128,128]{2,1,0:T(8,128)(2,1)S(1)}, bf16[32,128,128]{2,1,0:T(8,128)(2,1)S(1)}, u32[]{:S(2)}, u32[]{:S(2)}) collective-permute-start(bf16[32,128,128]{2,1,0:T(8,128)(2,1)S(1)} %pad_maximum_fusion.1.refs_1_), channel_id=1, source_target_pairs={{0,2},{2,4},{4,6},{6,0},{1,3},{3,5},{5,7},{7,1},{8,10},{10,12},{12... | collective-permute-start | bytes 3145736 | tf_op jit(solution)/shard_map/ppermute | solution.py:39
  41.2 24.7 %collective-permute-start.10 = (bf16[528,256]{1,0:T(8,128)(2,1)}, bf16[528,256]{1,0:T(8,128)(2,1)S(1)}, u32[]{:S(2)}, u32[]{:S(2)}) collective-permute-start(bf16[528,256]{1,0:T(8,128)(2,1)} %copy-done.18), channel_id=1, source_target_pairs={{0,8},{8,16},{16,24},{24,32},{32,40},{40,48},{48,56},{56,0},{1,9},... | collective-permute-start | bytes 811016 | tf_op jit(solution)/shard_map/ppermute | solution.py:39
  41.2 24.7 %collective-permute-start.11 = (bf16[528,256]{1,0:T(8,128)(2,1)}, bf16[528,256]{1,0:T(8,128)(2,1)S(1)}, u32[]{:S(2)}, u32[]{:S(2)}) collective-permute-start(bf16[528,256]{1,0:T(8,128)(2,1)} %copy-done.22), channel_id=1, source_target_pairs={{0,56},{8,0},{16,8},{24,16},{32,24},{40,32},{48,40},{56,48},{1,57}... | collective-permute-start | bytes 811016 | tf_op jit(solution)/shard_map/ppermute | solution.py:39
  65.9 7.2 %collective-permute-start.16 = (bf16[528,256]{1,0:T(8,128)(2,1)S(1)}, bf16[528,256]{1,0:T(8,128)(2,1)}, u32[]{:S(2)}, u32[]{:S(2)}) collective-permute-start(bf16[528,256]{1,0:T(8,128)(2,1)S(1)} %collective-permute-done.10.refs_6_.refs_15_), channel_id=1, source_target_pairs={{0,8},{8,16},{16,24},{24,32},{32,40},{40,48},{48,56},{56,0},{1,9},... | collective-permute-start | bytes 811016 | tf_op jit(solution)/shard_map/ppermute | solution.py:39
  66.6 6.4 %collective-permute-start.17 = (bf16[528,256]{1,0:T(8,128)(2,1)S(1)}, bf16[528,256]{1,0:T(8,128)(2,1)}, u32[]{:S(2)}, u32[]{:S(2)}) collective-permute-start(bf16[528,256]{1,0:T(8,128)(2,1)S(1)} %collective-permute-done.11.refs_2_.refs_10_), channel_id=1, source_target_pairs={{0,56},{8,0},{16,8},{24,16},{32,24},{40,32},{48,40},{56,48},{1,57}... | collective-permute-start | bytes 811016 | tf_op jit(solution)/shard_map/ppermute | solution.py:39
  70.2 6.7 %collective-permute-start.14 = (bf16[528,256]{1,0:T(8,128)(2,1)S(1)}, bf16[528,256]{1,0:T(8,128)(2,1)}, u32[]{:S(2)}, u32[]{:S(2)}) collective-permute-start(bf16[528,256]{1,0:T(8,128)(2,1)S(1)} %shard_map.192.refs_0_.refs_8_), channel_id=1, source_target_pairs={{0,64},{64,128},{128,192},{192,0},{1,65},{65,129},{129,193},{193,1... | collective-permute-start | bytes 811016 | tf_op jit(solution)/shard_map/ppermute | solution.py:39
  73.1 126.7 %all-gather.5.cloned.1.call-start = ((), (), s32[]{:S(2)}) async-start(), calls=%async_computation.4 | async-start | bytes 1253376 | tf_op jit(solution)/shard_map/all_gather | solution.py:530
  78.4 10.6 %collective-permute-start.20 = (bf16[16,128,128]{2,1,0:T(8,128)(2,1)S(1)}, bf16[16,128,128]{2,1,0:T(8,128)(2,1)S(1)}, u32[]{:S(2)}, u32[]{:S(2)}) collective-permute-start(bf16[16,128,128]{2,1,0:T(8,128)(2,1)S(1)} %slice.269), channel_id=1, source_target_pairs={{0,2},{2,4},{4,6},{6,0},{1,3},{3,5},{5,7},{7,1},{8,10},{10,12},{12... | collective-permute-start | bytes 1572872 | tf_op jit(solution)/shard_map/ppermute | solution.py:39
  78.6 10.5 %collective-permute-start.21 = (bf16[16,128,128]{2,1,0:T(8,128)(2,1)S(1)}, bf16[16,128,128]{2,1,0:T(8,128)(2,1)S(1)}, u32[]{:S(2)}, u32[]{:S(2)}) collective-permute-start(bf16[16,128,128]{2,1,0:T(8,128)(2,1)S(1)} %slice.270), channel_id=1, source_target_pairs={{0,6},{2,0},{4,2},{6,4},{1,7},{3,1},{5,3},{7,5},{8,14},{10,8},{12,... | collective-permute-start | bytes 1572872 | tf_op jit(solution)/shard_map/ppermute | solution.py:39
  82.2 6.8 %collective-permute-start.22 = (bf16[528,256]{1,0:T(8,128)(2,1)S(1)}, bf16[528,256]{1,0:T(8,128)(2,1)S(1)}, u32[]{:S(2)}, u32[]{:S(2)}) collective-permute-start(bf16[528,256]{1,0:T(8,128)(2,1)S(1)} %shard_map.192.refs_0_.refs_8_), channel_id=1, source_target_pairs={{0,128},{64,192},{128,0},{192,64},{1,129},{65,193},{129,1},{193,65... | collective-permute-start | bytes 811016 | tf_op jit(solution)/shard_map/ppermute | solution.py:39
  84.8 6.0 %collective-permute-start.18 = (bf16[272,256]{1,0:T(8,128)(2,1)S(1)}, bf16[272,256]{1,0:T(8,128)(2,1)S(1)}, u32[]{:S(2)}, u32[]{:S(2)}) collective-permute-start(bf16[272,256]{1,0:T(8,128)(2,1)S(1)} %slice.267), channel_id=1, source_target_pairs={{0,8},{8,16},{16,24},{24,32},{32,40},{40,48},{48,56},{56,0},{1,9},... | collective-permute-start | bytes 417800 | tf_op jit(solution)/shard_map/ppermute | solution.py:39
  107.8 32.3 %collective-permute-start.25 = (bf16[8,128,256]{2,1,0:T(8,128)(2,1)}, bf16[8,128,256]{2,1,0:T(8,128)(2,1)}, u32[]{:S(2)}, u32[]{:S(2)}) collective-permute-start(bf16[8,128,256]{2,1,0:T(8,128)(2,1)} %copy-done.80), channel_id=1, source_target_pairs={{0,2},{2,4},{4,6},{6,0},{1,3},{3,5},{5,7},{7,1},{8,10},{10,12},{12... | collective-permute-start | bytes 1572872 | tf_op jit(solution)/shard_map/ppermute | solution.py:39
  107.8 32.3 %collective-permute-start.26 = (bf16[8,128,256]{2,1,0:T(8,128)(2,1)}, bf16[8,128,256]{2,1,0:T(8,128)(2,1)}, u32[]{:S(2)}, u32[]{:S(2)}) collective-permute-start(bf16[8,128,256]{2,1,0:T(8,128)(2,1)} %copy-done.79), channel_id=1, source_target_pairs={{0,6},{2,0},{4,2},{6,4},{1,7},{3,1},{5,3},{7,5},{8,14},{10,8},{12,... | collective-permute-start | bytes 1572872 | tf_op jit(solution)/shard_map/ppermute | solution.py:39
  110.7 29.5 %collective-permute-start.27 = (bf16[8,128,256]{2,1,0:T(8,128)(2,1)}, bf16[8,128,256]{2,1,0:T(8,128)(2,1)}, u32[]{:S(2)}, u32[]{:S(2)}) collective-permute-start(bf16[8,128,256]{2,1,0:T(8,128)(2,1)} %copy-done.78), channel_id=1, source_target_pairs={{0,64},{64,128},{128,192},{192,0},{1,65},{65,129},{129,193},{193,1... | collective-permute-start | bytes 1572872 | tf_op jit(solution)/shard_map/ppermute | solution.py:39
  111.2 28.9 %collective-permute-start.23 = (bf16[4,128,256]{2,1,0:T(8,128)(2,1)}, bf16[4,128,256]{2,1,0:T(8,128)(2,1)}, u32[]{:S(2)}, u32[]{:S(2)}) collective-permute-start(bf16[4,128,256]{2,1,0:T(8,128)(2,1)} %copy-done.82), channel_id=1, source_target_pairs={{0,8},{8,16},{16,24},{24,32},{32,40},{40,48},{48,56},{56,0},{1,9},... | collective-permute-start | bytes 786440 | tf_op jit(solution)/shard_map/ppermute | solution.py:39
  111.4 28.8 %collective-permute-start.24 = (bf16[4,128,256]{2,1,0:T(8,128)(2,1)}, bf16[4,128,256]{2,1,0:T(8,128)(2,1)}, u32[]{:S(2)}, u32[]{:S(2)}) collective-permute-start(bf16[4,128,256]{2,1,0:T(8,128)(2,1)} %copy-done.81), channel_id=1, source_target_pairs={{0,56},{8,0},{16,8},{24,16},{32,24},{40,32},{48,40},{56,48},{1,57}... | collective-permute-start | bytes 786440 | tf_op jit(solution)/shard_map/ppermute | solution.py:39
  140.1 126.5 %all-gather.7.cloned.1.call-start = ((), (), s32[]{:S(2)}) async-start(), calls=%async_computation.5 | async-start | bytes 1769472 | tf_op jit(solution)/shard_map/all_gather | solution.py:532
  142.4 31.8 %collective-permute-start.28 = (bf16[8,128,256]{2,1,0:T(8,128)(2,1)S(1)}, bf16[8,128,256]{2,1,0:T(8,128)(2,1)S(1)}, u32[]{:S(2)}, u32[]{:S(2)}) collective-permute-start(bf16[8,128,256]{2,1,0:T(8,128)(2,1)S(1)} %pad_maximum_fusion.6), channel_id=1, source_target_pairs={{0,8},{8,16},{16,24},{24,32},{32,40},{40,48},{48,56},{56,0},{1,9},... | collective-permute-start | bytes 1572872 | tf_op jit(solution)/shard_map/ppermute | solution.py:39
  152.5 21.7 %collective-permute-start.29 = (bf16[8,128,256]{2,1,0:T(8,128)(2,1)S(1)}, bf16[8,128,256]{2,1,0:T(8,128)(2,1)S(1)}, u32[]{:S(2)}, u32[]{:S(2)}) collective-permute-start(bf16[8,128,256]{2,1,0:T(8,128)(2,1)S(1)} %pad_maximum_fusion.7), channel_id=1, source_target_pairs={{0,56},{8,0},{16,8},{24,16},{32,24},{40,32},{48,40},{56,48},{1,57}... | collective-permute-start | bytes 1572872 | tf_op jit(solution)/shard_map/ppermute | solution.py:39
  155.2 19.0 %collective-permute-start.30 = (bf16[8,128,256]{2,1,0:T(8,128)(2,1)S(1)}, bf16[8,128,256]{2,1,0:T(8,128)(2,1)S(1)}, u32[]{:S(2)}, u32[]{:S(2)}) collective-permute-start(bf16[8,128,256]{2,1,0:T(8,128)(2,1)S(1)} %copy-done.77), channel_id=1, source_target_pairs={{0,192},{64,0},{128,64},{192,128},{1,193},{65,1},{129,65},{193,129... | collective-permute-start | bytes 1572872 | tf_op jit(solution)/shard_map/ppermute | solution.py:39
  161.9 19.9 %collective-permute-start.33 = (bf16[16,128,256]{2,1,0:T(8,128)(2,1)S(1)}, bf16[16,128,256]{2,1,0:T(8,128)(2,1)}, u32[]{:S(2)}, u32[]{:S(2)}) collective-permute-start(bf16[16,128,256]{2,1,0:T(8,128)(2,1)S(1)} %pad_maximum_fusion.2), channel_id=1, source_target_pairs={{0,2},{2,4},{4,6},{6,0},{1,3},{3,5},{5,7},{7,1},{8,10},{10,12},{12... | collective-permute-start | bytes 3145736 | tf_op jit(solution)/shard_map/ppermute | solution.py:39
  163.6 18.3 %collective-permute-start.34 = (bf16[16,128,256]{2,1,0:T(8,128)(2,1)S(1)}, bf16[16,128,256]{2,1,0:T(8,128)(2,1)}, u32[]{:S(2)}, u32[]{:S(2)}) collective-permute-start(bf16[16,128,256]{2,1,0:T(8,128)(2,1)S(1)} %pad_maximum_fusion.3), channel_id=1, source_target_pairs={{0,6},{2,0},{4,2},{6,4},{1,7},{3,1},{5,3},{7,5},{8,14},{10,8},{12,... | collective-permute-start | bytes 3145736 | tf_op jit(solution)/shard_map/ppermute | solution.py:39
  176.3 23.4 %collective-permute-start.35 = (bf16[16,128,256]{2,1,0:T(8,128)(2,1)S(1)}, bf16[16,128,256]{2,1,0:T(8,128)(2,1)}, u32[]{:S(2)}, u32[]{:S(2)}) collective-permute-start(bf16[16,128,256]{2,1,0:T(8,128)(2,1)S(1)} %pad_maximum_fusion.4), channel_id=1, source_target_pairs={{0,64},{64,128},{128,192},{192,0},{1,65},{65,129},{129,193},{193,1... | collective-permute-start | bytes 3145736 | tf_op jit(solution)/shard_map/ppermute | solution.py:39
  176.6 10.0 %collective-permute-start.31 = (bf16[8,128,256]{2,1,0:T(8,128)(2,1)S(1)}, bf16[8,128,256]{2,1,0:T(8,128)(2,1)}, u32[]{:S(2)}, u32[]{:S(2)}) collective-permute-start(bf16[8,128,256]{2,1,0:T(8,128)(2,1)S(1)} %add_convert_fusion.7), channel_id=1, source_target_pairs={{0,8},{8,16},{16,24},{24,32},{32,40},{40,48},{48,56},{56,0},{1,9},... | collective-permute-start | bytes 1572872 | tf_op jit(solution)/shard_map/ppermute | solution.py:39
  178.2 8.5 %collective-permute-start.32 = (bf16[8,128,256]{2,1,0:T(8,128)(2,1)S(1)}, bf16[8,128,256]{2,1,0:T(8,128)(2,1)}, u32[]{:S(2)}, u32[]{:S(2)}) collective-permute-start(bf16[8,128,256]{2,1,0:T(8,128)(2,1)S(1)} %add_convert_fusion.6), channel_id=1, source_target_pairs={{0,56},{8,0},{16,8},{24,16},{32,24},{40,32},{48,40},{56,48},{1,57}... | collective-permute-start | bytes 1572872 | tf_op jit(solution)/shard_map/ppermute | solution.py:39
  201.9 44.0 %collective-permute-start.42 = (bf16[16,128,256]{2,1,0:T(8,128)(2,1)S(1)}, bf16[16,128,256]{2,1,0:T(8,128)(2,1)S(1)}, u32[]{:S(2)}, u32[]{:S(2)}) collective-permute-start(bf16[16,128,256]{2,1,0:T(8,128)(2,1)S(1)} %pad_maximum_fusion.5), channel_id=1, source_target_pairs={{0,192},{64,0},{128,64},{192,128},{1,193},{65,1},{129,65},{193,129... | collective-permute-start | bytes 3145736 | tf_op jit(solution)/shard_map/ppermute | solution.py:39
  204.1 5.9 %collective-permute-start.38 = (bf16[1,128,256]{2,1,0:T(8,128)(2,1)S(1)}, bf16[1,128,256]{2,1,0:T(8,128)(2,1)S(1)}, u32[]{:S(2)}, u32[]{:S(2)}) collective-permute-start(bf16[1,128,256]{2,1,0:T(8,128)(2,1)S(1)} %get-tuple-element.216), channel_id=1, source_target_pairs={{0,56},{8,0},{16,8},{24,16},{32,24},{40,32},{48,40},{56,48},{1,57}... | collective-permute-start | bytes 196616 | tf_op jit(solution)/shard_map/ppermute | solution.py:39
  209.9 36.0 %collective-permute-start.41 = (bf16[8,128,256]{2,1,0:T(8,128)(2,1)S(1)}, bf16[8,128,256]{2,1,0:T(8,128)(2,1)S(1)}, u32[]{:S(2)}, u32[]{:S(2)}) collective-permute-start(bf16[8,128,256]{2,1,0:T(8,128)(2,1)S(1)} %add_convert_fusion.1), channel_id=1, source_target_pairs={{0,56},{8,0},{16,8},{24,16},{32,24},{40,32},{48,40},{56,48},{1,57}... | collective-permute-start | bytes 1572872 | tf_op jit(solution)/shard_map/ppermute | solution.py:39
  210.1 17.4 %collective-permute-start.39 = (bf16[2,128,256]{2,1,0:T(8,128)(2,1)S(1)}, bf16[2,128,256]{2,1,0:T(8,128)(2,1)S(1)}, u32[]{:S(2)}, u32[]{:S(2)}) collective-permute-start(bf16[2,128,256]{2,1,0:T(8,128)(2,1)S(1)} %pad_maximum_fusion.12), channel_id=1, source_target_pairs={{0,56},{8,0},{16,8},{24,16},{32,24},{40,32},{48,40},{56,48},{1,57}... | collective-permute-start | bytes 393224 | tf_op jit(solution)/shard_map/ppermute | solution.py:39
  214.3 31.5 %collective-permute-start.40 = (bf16[8,128,256]{2,1,0:T(8,128)(2,1)S(1)}, bf16[8,128,256]{2,1,0:T(8,128)(2,1)S(1)}, u32[]{:S(2)}, u32[]{:S(2)}) collective-permute-start(bf16[8,128,256]{2,1,0:T(8,128)(2,1)S(1)} %add_convert_fusion.2), channel_id=1, source_target_pairs={{0,8},{8,16},{16,24},{24,32},{32,40},{40,48},{48,56},{56,0},{1,9},... | collective-permute-start | bytes 1572872 | tf_op jit(solution)/shard_map/ppermute | solution.py:39
  214.6 20.9 %collective-permute-start.36 = (bf16[1,128,256]{2,1,0:T(8,128)(2,1)S(1)}, bf16[1,128,256]{2,1,0:T(8,128)(2,1)S(1)}, u32[]{:S(2)}, u32[]{:S(2)}) collective-permute-start(bf16[1,128,256]{2,1,0:T(8,128)(2,1)S(1)} %get-tuple-element.217), channel_id=1, source_target_pairs={{0,8},{8,16},{16,24},{24,32},{32,40},{40,48},{48,56},{56,0},{1,9},... | collective-permute-start | bytes 196616 | tf_op jit(solution)/shard_map/ppermute | solution.py:39
  235.6 9.2 %collective-permute-start.37 = (bf16[2,128,256]{2,1,0:T(8,128)(2,1)S(1)}, bf16[2,128,256]{2,1,0:T(8,128)(2,1)S(1)}, u32[]{:S(2)}, u32[]{:S(2)}) collective-permute-start(bf16[2,128,256]{2,1,0:T(8,128)(2,1)S(1)} %pad_maximum_fusion.11), channel_id=1, source_target_pairs={{0,8},{8,16},{16,24},{24,32},{32,40},{40,48},{48,56},{56,0},{1,9},... | collective-permute-start | bytes 393224 | tf_op jit(solution)/shard_map/ppermute | solution.py:39
  247.1 7.8 %collective-permute-start.44 = (bf16[2,128,256]{2,1,0:T(8,128)(2,1)S(1)}, bf16[2,128,256]{2,1,0:T(8,128)(2,1)S(1)}, u32[]{:S(2)}, u32[]{:S(2)}) collective-permute-start(bf16[2,128,256]{2,1,0:T(8,128)(2,1)S(1)} %get-tuple-element.183), channel_id=1, source_target_pairs={{0,56},{8,0},{16,8},{24,16},{32,24},{40,32},{48,40},{56,48},{1,57}... | collective-permute-start | bytes 393224 | tf_op jit(solution)/shard_map/ppermute | solution.py:39
  247.2 7.8 %collective-permute-start.43 = (bf16[2,128,256]{2,1,0:T(8,128)(2,1)S(1)}, bf16[2,128,256]{2,1,0:T(8,128)(2,1)S(1)}, u32[]{:S(2)}, u32[]{:S(2)}) collective-permute-start(bf16[2,128,256]{2,1,0:T(8,128)(2,1)S(1)} %add_convert_fusion.19), channel_id=1, source_target_pairs={{0,8},{8,16},{16,24},{24,32},{32,40},{40,48},{48,56},{56,0},{1,9},... | collective-permute-start | bytes 393224 | tf_op jit(solution)/shard_map/ppermute | solution.py:39
  256.9 5.8 %collective-permute-start.50 = (bf16[4,128,256]{2,1,0:T(8,128)(2,1)S(1)}, bf16[4,128,256]{2,1,0:T(8,128)(2,1)S(1)}, u32[]{:S(2)}, u32[]{:S(2)}) collective-permute-start(bf16[4,128,256]{2,1,0:T(8,128)(2,1)S(1)} %get-tuple-element.188), channel_id=1, source_target_pairs={{0,6},{2,0},{4,2},{6,4},{1,7},{3,1},{5,3},{7,5},{8,14},{10,8},{12,... | collective-permute-start | bytes 786440 | tf_op jit(solution)/shard_map/ppermute | solution.py:39
  259.3 6.4 %collective-permute-start.49 = (bf16[4,128,256]{2,1,0:T(8,128)(2,1)S(1)}, bf16[4,128,256]{2,1,0:T(8,128)(2,1)S(1)}, u32[]{:S(2)}, u32[]{:S(2)}) collective-permute-start(bf16[4,128,256]{2,1,0:T(8,128)(2,1)S(1)} %get-tuple-element.187), channel_id=1, source_target_pairs={{0,2},{2,4},{4,6},{6,0},{1,3},{3,5},{5,7},{7,1},{8,10},{10,12},{12... | collective-permute-start | bytes 786440 | tf_op jit(solution)/shard_map/ppermute | solution.py:39
  266.5 22.1 %collective-permute-start.52 = (f32[8,4,32,384]{3,2,1,0:T(8,128)}, f32[8,4,32,384]{3,2,1,0:T(8,128)S(1)}, u32[]{:S(2)}, u32[]{:S(2)}) collective-permute-start(f32[8,4,32,384]{3,2,1,0:T(8,128)} %bitcast.52), channel_id=1, source_target_pairs={{0,1},{1,0},{2,3},{3,2},{4,5},{5,4},{6,7},{7,6},{8,9},{9,8},{10,11... | collective-permute-start | bytes 4718600 | tf_op jit(solution)/shard_map/ppermute | solution.py:39
  279.6 6.7 %collective-permute-start.51 = (f32[2,128,256]{2,1,0:T(8,128)}, f32[2,128,256]{2,1,0:T(8,128)S(1)}, u32[]{:S(2)}, u32[]{:S(2)}) collective-permute-start(f32[2,128,256]{2,1,0:T(8,128)} %slice.378), channel_id=1, source_target_pairs={{0,1},{1,0},{2,3},{3,2},{4,5},{5,4},{6,7},{7,6},{8,9},{9,8},{10,11... | collective-permute-start | bytes 786440 | tf_op jit(solution)/shard_map/ppermute | solution.py:39
  (98 other events, 624.2 us)
Sparse Core Ops, SparseCore 0:
  39.7 26.6 reduce-scatter.2
  73.2 33.7 reduce-scatter.4
  140.2 56.1 all-gather.4
  201.7 43.4 all-gather.6
